TPU v7x, 32 devices: a whole 2x2x4 slice. The times are simulated.
32 devices in a mesh: tm: 16 (over z, x, core), head: 2 (over y).
Axes of the slice: x: 2, y: 2, z: 4, core: 2. Of those that a mesh axis runs over, the one named last changes fastest.
Arguments:
- query_states: bfloat16 [24576, 1024], P('tm', 'head'), may hold values from -30 to 30
- key_states: bfloat16 [24576, 1024], P('tm', 'head'), may hold values from -30 to 30
- value_states: bfloat16 [24576, 1024], P('tm', 'head'), may hold values from -6 to 6
- win_start: int32 [32], P('tm'), may hold values from 0 to 30, as said below
- group_end: int32 [32], P('tm'), may hold values from 0 to 31, as said below
- out_weight: bfloat16 [1024, 1536], replicated, may hold values from -0.1875 to 0.1875
Outputs:
- projected: bfloat16 [24576, 1536], P(('tm', 'head'))
Inputs may be any that keep to these rules, and one draw needn't show every extreme that they name: For every frame f, win_start[f] = max(f - lag, 0) with a lag of 1 to 3; frame 32 - 2 has a lag of 3 in every draw, and the last frame has a lag of 1. `group_end`: frames 2p and 2p + 1 form one group (both end at 2p + 1) or two groups of one frame (each ends at itself); both kinds occur in every draw.
All inputs are finite; a program needn't handle non-finite values.
Results may differ from a plain program's by a relative error of at most 0.0051.
Values may be sent and summed in bfloat16 or wider, within the bound.
No kernel may reach another device: no remote copies, remote signals or barrier semaphores. Data moves between devices by JAX's collectives and lax.ppermute only.
A program may use at most 384 MiB of HBM per device.

v0:
```python
import jax
import jax.numpy as jnp
from jax import lax
from jax.sharding import PartitionSpec as P

HD = 128
FT = 768


def spread(block, axis, owner):
    block = jnp.where(lax.axis_index(axis) == owner, block, jnp.zeros_like(block))
    return lax.psum(block, axis)


def from_behind(array, axis, by):
    length = lax.axis_size(axis)
    pairs = [(i, i + by) for i in range(length) if 0 <= i + by < length]
    return lax.ppermute(array, axis, pairs)


def attend(query_rows, key_rows, value_rows, visible):
    heads_here = query_rows.shape[1] // HD
    query_heads = query_rows.reshape(query_rows.shape[0], heads_here, HD)
    key_heads = key_rows.reshape(key_rows.shape[0], heads_here, HD)
    value_heads = value_rows.reshape(value_rows.shape[0], heads_here, HD)
    scores = jnp.einsum(
        "qhd,khd->hqk", query_heads, key_heads, preferred_element_type=jnp.float32
    ) * HD ** (-0.5)
    scores = jnp.where(visible[None, None, :], scores, -1e30)
    peak = jnp.max(scores, axis=-1, keepdims=True)
    weights = jnp.where(visible[None, None, :], jnp.exp(scores - peak), 0.0)
    total = jnp.sum(weights, axis=-1)
    rounded = weights.astype(jnp.bfloat16)
    mixed = jnp.einsum("hqk,khd->qhd", rounded, value_heads, preferred_element_type=jnp.float32)
    mixed = mixed / jnp.transpose(total)[:, :, None]
    return mixed.astype(jnp.bfloat16).reshape(query_rows.shape[0], query_rows.shape[1])


def local(query_states, key_states, value_states, win_start, group_end, out_weight):
    local_frames = win_start.shape[0]
    stacked = jnp.stack([key_states, value_states])
    sink_frame = stacked[:, :FT]
    sink_states = spread(sink_frame, "tm", 0)
    near_count = min(3, local_frames)
    far_count = 3 - near_count
    near_frames = from_behind(stacked, "tm", 1)
    pieces = []
    far_frames = from_behind(stacked[:, (local_frames - far_count) * FT :], "tm", 2)
    pieces.append(far_frames)
    extended = jnp.concatenate(pieces + [near_frames, stacked], axis=1)
    first_id = lax.axis_index("tm") * local_frames - 3
    outputs = []
    for slot in range(local_frames):
        span_frames = 5 if slot % 2 == 0 else 4
        window = extended[:, slot * FT : (slot + span_frames) * FT]
        key_rows = jnp.concatenate([sink_states[0], window[0]], axis=0)
        value_rows = jnp.concatenate([sink_states[1], window[1]], axis=0)
        frame_ids = first_id + slot + jnp.arange(span_frames * FT, dtype=jnp.int32) // FT
        window_seen = (
            (frame_ids >= 1) & (frame_ids >= win_start[slot]) & (frame_ids <= group_end[slot])
        )
        visible = jnp.concatenate([jnp.ones((FT,), dtype=bool), window_seen])
        query_rows = query_states[slot * FT : (slot + 1) * FT]
        outputs.append(attend(query_rows, key_rows, value_rows, visible))
    attended = jnp.concatenate(outputs, axis=0)
    token_rows = lax.all_to_all(attended, "head", split_axis=0, concat_axis=1, tiled=True)
    return jnp.dot(token_rows, out_weight, preferred_element_type=jnp.float32).astype(jnp.bfloat16)


def solution(mesh):
    in_specs = (P("tm", "head"), P("tm", "head"), P("tm", "head"), P("tm"), P("tm"), P())
    out_specs = P(("tm", "head"), None)
    return jax.shard_map(local, mesh=mesh, in_specs=in_specs, out_specs=out_specs, check_vma=False)
```

profile of v0, /device:TPU:18, one launch (start us, length us, event | category | flops | bytes accessed | tf_op | source)
XLA Modules:
  0.0 491.1 jit_solution(18268910754415849769)
XLA Ops:
  6.5 2.8 copy.24
  11.9 3.8 pad_maximum_fusion
  17.8 3.2 fusion.34
  21.0 3.4 collective-permute-start
  28.3 2.7 fusion.64
  35.6 92.8 %all-reduce.4.cloned.1.call-done = bf16[2,768,512]{1,2,0:T(8,128)(2,1)} async-done(((bf16[2,768,512]{1,2,0:T(8,128)(2,1)}), bf16[2,768,512]{1,2,0:T(8,128)(2,1)}) %all-reduce.4.cloned.1.call-update) | async-done | bytes 1572880 | tf_op jit(solution)/shard_map/psum | solution.py:12
  133.3 4.0 maximum_maximum_fusion
  137.3 3.4 fusion.62
  140.7 6.3 %copy.27 = bf16[3840,4,128]{2,0,1:T(8,128)(2,1)} copy(bf16[3840,4,128]{0,2,1:T(8,128)(2,1)} %bitcast.70) | data formatting | bytes 7864320 | tf_op jit(solution)/shard_map/concatenate | solution.py:56
  147.0 3.7 maximum_maximum_fusion.1
  150.6 3.0 fusion.63
  153.7 4.7 copy.32
  158.3 30.2 %fusion.68 = (f32[4,768]{1,0:T(4,128)S(1)}, bf16[4,768,3840]{1,2,0:T(8,128)(2,1)}) fusion(pred[3840]{0:T(1024)(128)(4,1)S(1)} %concatenate.54, bf16[768,4,128]{0,2,1:T(8,128)(2,1)} %bitcast.79, bf16[3072,4,128]{2,0,1:T(8,128)(2,1)} %copy.32, bf16[768,4,128]{2,0,1:T(8,128)(2,1)} %copy.26), kind=kOutput, calls=%fused_computation.81 | convolution fusion | flops 3098545920 | bytes 28327680 | tf_op jit(solution)/shard_map/sub | solution.py:31
  188.5 13.0 %fusion.35 = bf16[768,4,128]{0,2,1:T(8,128)(2,1)} fusion(bf16[4,768,3840]{1,2,0:T(8,128)(2,1)} %get-tuple-element.20, bf16[3072,4,128]{0,2,1:T(8,128)(2,1)} %bitcast.77, bf16[768,4,128]{0,2,1:T(8,128)(2,1)} %bitcast.82, f32[768,4]{0,1:T(4,128)S(1)} %bitcast.85), kind=kOutput, calls=%fused_computation.47 | convolution fusion | flops 3028549632 | bytes 28323840 | tf_op jit(solution)/shard_map/hqk,khd->qhd/dot_general | solution.py:34
  203.8 22.9 %fusion.24 = f32[4,4608,768]{2,1,0:T(8,128)} fusion(bf16[768,4,128]{0,2,1:T(8,128)(2,1)} %bitcast.75, bf16[3840,4,128]{2,0,1:T(8,128)(2,1)} %copy.27, bf16[768,4,128]{2,0,1:T(8,128)(2,1)} %copy.26), kind=kOutput, calls=%fused_computation.27 | convolution fusion | flops 3633315840 | bytes 62128128 | tf_op jit(solution)/shard_map/qhd,khd->hqk/dot_general | solution.py:26
  226.7 7.1 %broadcast_in_dim.53 = pred[4,4608,768]{2,1,0:T(8,128)(4,1)} broadcast(pred[4608]{0:T(1024)(128)(4,1)S(1)} %concatenate.47), dimensions={1} | broadcast | bytes 14160384 | tf_op jit(solution)/shard_map/jit(_where)/broadcast_in_dim | solution.py:31
  233.8 7.1 %broadcast_in_dim.52 = pred[4,768,4608]{1,2,0:T(8,128)(4,1)} broadcast(pred[4608]{0:T(1024)(128)(4,1)S(1)} %concatenate.47), dimensions={2} | broadcast | bytes 14160384 | tf_op jit(solution)/shard_map/jit(_where)/broadcast_in_dim | solution.py:31
  240.9 18.0 %mul.18 = f32[4,4608,768]{2,1,0:T(8,128)} broadcast(f32[]{:T(128)} %constant.41.clone.1), dimensions={} | broadcast | bytes 56623108 | tf_op jit(solution)/shard_map/mul | solution.py:26
  258.9 18.0 %broadcast_in_dim.54 = f32[4,4608,768]{2,1,0:T(8,128)} broadcast(f32[]{:T(128)} %constant.42.clone.1), dimensions={} | broadcast | bytes 56623108 | tf_op jit(solution)/shard_map/jit(_where)/broadcast_in_dim | solution.py:29
  276.9 18.1 %broadcast_in_dim.55 = f32[4,768,4608]{1,2,0:T(8,128)} broadcast(f32[]{:T(128)} %constant.44.clone.1), dimensions={} | broadcast | bytes 56623108 | tf_op jit(solution)/shard_map/jit(_where)/broadcast_in_dim | solution.py:31
  295.0 141.4 %fusion.69 = (f32[4,768]{1,0:T(4,128)S(1)}, bf16[4,768,4608]{1,2,0:T(8,128)(2,1)}) fusion(pred[4,768,4608]{1,2,0:T(8,128)(4,1)} %broadcast_in_dim.52, f32[4,768,4608]{1,2,0:T(8,128)} %broadcast_in_dim.55, pred[4,4608,768]{2,1,0:T(8,128)(4,1)} %broadcast_in_dim.53, f32[4,4608,768]{2,1,0:T(8,128)} %broadcast_in_dim.54, f32[4,4608,768]{2,1,0:T(8,128)} %fusion.24, ...), kind=kOutput, calls=%fused_computation.82 | output fusion | flops 113250816 | bytes 283127808 | tf_op jit(solution)/shard_map/sub | solution.py:31
  436.4 15.2 %fusion.36 = bf16[768,4,128]{0,2,1:T(8,128)(2,1)} fusion(bf16[4,768,4608]{1,2,0:T(8,128)(2,1)} %get-tuple-element.22, bf16[3840,4,128]{0,2,1:T(8,128)(2,1)} %bitcast.74, bf16[768,4,128]{0,2,1:T(8,128)(2,1)} %bitcast.83, f32[768,4]{0,1:T(4,128)S(1)} %bitcast.84), kind=kOutput, calls=%fused_computation.49 | convolution fusion | flops 3634102272 | bytes 33828864 | tf_op jit(solution)/shard_map/hqk,khd->qhd/dot_general | solution.py:34
  455.4 20.9 %all_to_all.19 = bf16[2,768,512]{2,1,0:T(8,128)(2,1)} all-to-all(bf16[2,768,512]{2,1,0:T(8,128)(2,1)S(1)} %bitcast.72), channel_id=1, replica_groups=mesh['tm'=16,'head'=2] {'head'}, dimensions={0} | all-to-all | bytes 3145728 | tf_op jit(solution)/shard_map/all_to_all | solution.py:66
  478.9 5.3 %convolution_convert_fusion = bf16[768,1536]{1,0:T(8,128)(2,1)} fusion(bf16[768,1024]{0,1:T(8,128)(2,1)} %bitcast.78, bf16[1024,1536]{1,0:T(8,128)(2,1)S(1)} %copy-done), kind=kOutput, calls=%fused_computation.40 | convolution fusion | flops 2417098752 | bytes 7077888 | tf_op jit(solution)/shard_map/dot_general | solution.py:67
  (26 shorter events, 26.6 us)
Async XLA Ops:
  6.5 472.4 %copy-start = (bf16[1024,1536]{1,0:T(8,128)(2,1)S(1)}, bf16[1024,1536]{1,0:T(8,128)(2,1)}, u32[]{:S(2)}) copy-start(bf16[1024,1536]{1,0:T(8,128)(2,1)} %param.11) | copy-start | bytes 9437188
  6.5 121.9 %all-reduce.4.cloned.1.call-start = ((), (), s32[]{:S(2)}) async-start(), calls=%async_computation.1 | async-start | bytes 3145728 | tf_op jit(solution)/shard_map/psum | solution.py:12
  15.7 8.7 %copy-start.1 = (s32[2]{0:T(128)S(1)}, s32[2]{0:T(128)}, u32[]{:S(2)}) copy-start(s32[2]{0:T(128)} %param.9) | copy-start | bytes 28
  15.7 9.4 %copy-start.2 = (s32[2]{0:T(128)S(1)}, s32[2]{0:T(128)}, u32[]{:S(2)}) copy-start(s32[2]{0:T(128)} %param.10) | copy-start | bytes 28
  15.7 117.6 %collective-permute-start.1 = (bf16[2,1536,512]{1,2,0:T(8,128)(2,1)}, bf16[2,1536,512]{1,2,0:T(8,128)(2,1)}, u32[]{:S(2)}, u32[]{:S(2)}) collective-permute-start(bf16[2,1536,512]{1,2,0:T(8,128)(2,1)} %pad_maximum_fusion), channel_id=1, source_target_pairs={{0,2},{2,4},{4,6},{6,8},{8,10},{10,12},{12,14},{14,16},{16,18},{18... | collective-permute-start | bytes 9437192 | tf_op jit(solution)/shard_map/ppermute | solution.py:18
  21.0 112.3 %collective-permute-start = (bf16[2,768,512]{1,2,0:T(8,128)(2,1)}, bf16[2,768,512]{1,2,0:T(8,128)(2,1)}, u32[]{:S(2)}, u32[]{:S(2)}) collective-permute-start(bf16[2,768,512]{1,2,0:T(8,128)(2,1)} %get-tuple-element.9), channel_id=1, source_target_pairs={{0,4},{2,6},{4,8},{6,10},{8,12},{10,14},{12,16},{14,18},{16,20},{1... | collective-permute-start | bytes 4718600 | tf_op jit(solution)/shard_map/ppermute | solution.py:18
Sparse Core Ops, SparseCore 0:
  24.6 103.8 all-reduce.3
where the time goes:
time: 496 us; the launch traced here: 491 us
  other arithmetic  160 us (32%)
  local copies, waits for them, and re-layouts  112 us (23%)
  waiting for transfers between devices  92.8 us (19%)
  matrix products  86.6 us (17%)
  blocking collectives  20.9 us (4%)
  between operations  13.5 us (3%)
  starting transfers between devices  5.49 us (1%)
    sub x1, other arithmetic, attend(): weights = jnp.where(visible[None, None, :], jnp.exp(scores - peak), 0.0)  141 us
    psum x1, waiting for transfers between devices, spread(): return lax.psum(block, axis)  92.8 us
    broadcast_in_dim x3, local copies, waits for them, and re-layouts, attend(): weights = jnp.where(visible[None, None, :], jnp.exp(scores - peak), 0.0)  32.3 us
    sub x1, matrix products, attend(): weights = jnp.where(visible[None, None, :], jnp.exp(scores - peak), 0.0)  30.2 us
    dot_general x2, matrix products, attend(): jnp.einsum('hqk,khd->qhd', rounded, value_heads, preferred_element_type=j...  28.2 us
    dot_general x1, matrix products, attend(): jnp.einsum('qhd,khd->hqk', query_heads, key_heads, preferred_element_type...  22.9 us
    all_to_all x1, blocking collectives, local(): lax.all_to_all(attended, 'head', split_axis=0, concat_axis=1, tiled=True)  20.9 us
    mul x1, local copies, waits for them, and re-layouts, attend(): jnp.einsum('qhd,khd->hqk', query_heads, key_heads, preferred_element_type...  18 us
  transfers between devices with their start and end apart: 3, of which 1 were waited for; matrix products, arithmetic and copies ran while one was open for 4% of the time, Pallas kernels for 0%

commit v1 on v0

v1 whole, which is shorter than its diff:
```python
import functools

import jax
import jax.numpy as jnp
from jax import lax
from jax.experimental import pallas as pl
from jax.experimental.pallas import tpu as pltpu
from jax.sharding import PartitionSpec as P

HD = 128
FT = 768
BQ = 256
BK = 256
LOG2E = 1.4426950408889634
SCALE = HD ** -0.5 * LOG2E
LIMIT = 1e30


def qk(q, k):
    return lax.dot_general(q, k, (((1,), (1,)), ((), ())), preferred_element_type=jnp.float32)


def accumulate(q, k, v, m, acc, l):
    nq, nk = FT // BQ, FT // BK
    units = [(i, j) for i in range(nq) for j in range(nk)]

    def scores(unit):
        i, j = unit
        return qk(q[i * BQ : (i + 1) * BQ, :], k[j * BK : (j + 1) * BK, :])

    ahead = scores(units[0])
    for n, (i, j) in enumerate(units):
        s = ahead
        if n + 1 < len(units):
            ahead = scores(units[n + 1])
        rows = slice(i * BQ, (i + 1) * BQ)
        if j == 0:
            total = acc[rows, :]
            weight_sum = l[rows, :]
        shift = m[rows, :]
        parts = []
        for c in range(BK // 128):
            part = jnp.exp2(s[:, c * 128 : (c + 1) * 128] * SCALE - shift)
            weight_sum = weight_sum + part
            parts.append(part.astype(jnp.bfloat16))
        weights = jnp.concatenate(parts, axis=1)
        total = total + jnp.dot(
            weights, v[j * BK : (j + 1) * BK, :], preferred_element_type=jnp.float32
        )
        if j == nk - 1:
            acc[rows, :] = total
            l[rows, :] = weight_sum


def visible(info, slot, frame):
    return (frame >= 1) & (frame >= info[2 + slot]) & (frame <= info[4 + slot])


def local_kernel(info, q, k0, v0, k1, v1, m, acc, l):
    slot = pl.program_id(1)
    first = info[0]

    def start(k):
        for i in range(FT // BQ):
            rows = slice(i * BQ, (i + 1) * BQ)
            s = qk(q[rows, :], k[0:BK, :]) * SCALE
            m[rows, :] = jnp.broadcast_to(jnp.max(s, axis=1, keepdims=True), (BQ, 128))

    @pl.when(slot == 0)
    def _():
        start(k0)

    @pl.when(slot == 1)
    def _():
        start(k1)

    acc[...] = jnp.zeros_like(acc)
    l[...] = jnp.zeros_like(l)

    @pl.when(visible(info, slot, first))
    def _():
        accumulate(q, k0, v0, m, acc, l)

    @pl.when(visible(info, slot, first + 1))
    def _():
        accumulate(q, k1, v1, m, acc, l)


def near_kernel(info, q, k0, v0, k1, v1, m, acc_in, l_in, acc, l):
    slot = pl.program_id(1)
    first = info[0]
    acc[...] = acc_in[...]
    l[...] = l_in[...]

    @pl.when(visible(info, slot, first - 1))
    def _():
        accumulate(q, k1, v1, m, acc, l)

    @pl.when(visible(info, slot, first - 2))
    def _():
        accumulate(q, k0, v0, m, acc, l)


def final_kernel(
    info, q, sink_a, sink_b, far_k, far_v, relay_k, relay_v, m, acc_in, l_in,
    key_hbm, value_hbm, near_k_hbm, near_v_hbm, sink_a_hbm, sink_b_hbm, far_hbm, relay_hbm,
    out, acc, l, exact_m, k_buf, v_buf, sem,
):
    head = pl.program_id(0)
    slot = pl.program_id(1)
    first = info[0]
    core = info[6]
    acc[...] = acc_in[...]
    l[...] = l_in[...]

    @pl.when(core == 0)
    def _():
        accumulate(q, sink_a, sink_b, m, acc, l)

    @pl.when(core == 1)
    def _():
        accumulate(q, sink_b, sink_a, m, acc, l)

    far_seen = (slot == 0) & visible(info, slot, first - 3)

    @pl.when(far_seen & (core == 0))
    def _():
        accumulate(q, far_k, far_v, m, acc, l)

    @pl.when(far_seen & (core == 1))
    def _():
        accumulate(q, relay_k, relay_v, m, acc, l)

    total = jnp.sum(l[...], axis=1, keepdims=True)
    out[...] = (acc[...] / total).astype(out.dtype)
    in_range = jnp.max(total) < LIMIT

    @pl.when(jnp.logical_not(in_range))
    def _():
        columns = pl.ds(pl.multiple_of(head * HD, HD), HD)

        def sweep(step):
            def run(seen, k_hbm, v_hbm, k_row, v_row):
                @pl.when(seen)
                def _():
                    copies = (
                        pltpu.make_async_copy(
                            k_hbm.at[pl.ds(k_row, FT), columns], k_buf, sem.at[0]
                        ),
                        pltpu.make_async_copy(
                            v_hbm.at[pl.ds(v_row, FT), columns], v_buf, sem.at[1]
                        ),
                    )
                    for copy in copies:
                        copy.start()
                    for copy in copies:
                        copy.wait()
                    step()

            run(core == 0, sink_a_hbm, sink_b_hbm, 0, 0)
            run(core == 1, sink_b_hbm, sink_a_hbm, 0, 0)
            run(visible(info, slot, first), key_hbm, value_hbm, 0, 0)
            run(visible(info, slot, first + 1), key_hbm, value_hbm, FT, FT)
            run(visible(info, slot, first - 1), near_k_hbm, near_v_hbm, FT, FT)
            run(visible(info, slot, first - 2), near_k_hbm, near_v_hbm, 0, 0)
            run(far_seen & (core == 0), far_hbm, far_hbm, 0, FT)
            run(far_seen & (core == 1), relay_hbm, relay_hbm, 0, FT)

        def peak():
            for i in range(FT // BQ):
                rows = slice(i * BQ, (i + 1) * BQ)
                s = qk(q[rows, :], k_buf[...]) * SCALE
                here = jnp.max(s, axis=1, keepdims=True)
                exact_m[rows, :] = jnp.maximum(exact_m[rows, :], here)

        exact_m[...] = jnp.full_like(exact_m, -jnp.inf)
        sweep(peak)
        acc[...] = jnp.zeros_like(acc)
        l[...] = jnp.zeros_like(l)
        sweep(lambda: accumulate(q, k_buf, v_buf, exact_m, acc, l))
        out[...] = (acc[...] / jnp.sum(l[...], axis=1, keepdims=True)).astype(out.dtype)


def frame_spec(row_block):
    return pl.BlockSpec((FT, HD), lambda h, s, info: (row_block, h))


SLOT_SPEC = pl.BlockSpec((FT, HD), lambda h, s, info: (s, h))
HBM_SPEC = pl.BlockSpec(memory_space=pl.ANY)


def stage(kernel, info, heads, arrays, in_specs, out_shape, pairs, scratch=()):
    flops = int(pairs * heads * 4 * FT * FT * HD * 2)
    grid_spec = pltpu.PrefetchScalarGridSpec(
        num_scalar_prefetch=1,
        grid=(heads, 2),
        in_specs=in_specs,
        out_specs=jax.tree.map(lambda _: SLOT_SPEC, out_shape),
        scratch_shapes=list(scratch),
    )
    return pl.pallas_call(
        kernel,
        grid_spec=grid_spec,
        out_shape=out_shape,
        compiler_params=pltpu.CompilerParams(vmem_limit_bytes=48 * 1024 * 1024),
        cost_estimate=pl.CostEstimate(
            flops=flops, bytes_accessed=16_000_000, transcendentals=int(pairs * heads * FT * FT)
        ),
    )(info, *arrays)


def sink_from_first(key_rows, value_rows, axis):
    size = lax.axis_size(axis)
    me = lax.axis_index(axis)
    core = me % 2
    moved = lax.ppermute(value_rows, axis, [(0, 1)])
    held = jnp.where(core == 0, key_rows, moved)
    bits = [1 << b for b in range(1, size.bit_length() - 1)]
    orders = (bits[::-1], [bits[0]] + bits[:0:-1])
    done = [0, 0]
    for step in range(len(bits)):
        pairs = []
        for which in (0, 1):
            bit = orders[which][step]
            holders = [i for i in range(0, size, 2) if i & ~done[which] == 0]
            pairs += [(i + which, (i | bit) + which) for i in holders]
            done[which] |= bit
        moved = lax.ppermute(held, axis, pairs)
        takes = jnp.zeros((), bool)
        for _, target in pairs:
            takes = takes | (me == target)
        held = jnp.where(takes, moved, held)
    other = lax.ppermute(held, axis, [(i, i ^ 1) for i in range(size)])
    return held, other


def local(query_states, key_states, value_states, win_start, group_end, out_weight):
    axis = "tm"
    size = lax.axis_size(axis)
    me = lax.axis_index(axis)
    heads = query_states.shape[1] // HD
    first = me * 2
    info = jnp.concatenate(
        [
            jnp.stack([first, lax.axis_index("head")]).astype(jnp.int32),
            win_start.astype(jnp.int32),
            group_end.astype(jnp.int32),
            jnp.stack([me % 2]).astype(jnp.int32),
        ]
    )

    sink_a, sink_b = sink_from_first(key_states[:FT], value_states[:FT], axis)
    onward = [(i, i + 1) for i in range(size - 1)]
    near_k = lax.ppermute(key_states, axis, onward)
    near_v = lax.ppermute(value_states, axis, onward)
    own_last = jnp.concatenate([key_states[FT:], value_states[FT:]], axis=0)
    far = lax.ppermute(own_last, axis, [(i, i + 2) for i in range(0, size - 2, 2)])
    near_last = jnp.concatenate([near_k[FT:], near_v[FT:]], axis=0)
    relay = lax.ppermute(near_last, axis, [(i, i + 1) for i in range(0, size, 2)])

    rows, width = query_states.shape
    wide = jax.ShapeDtypeStruct((rows, width), jnp.float32)
    m, acc, l = stage(
        local_kernel, info, heads,
        [query_states, key_states, value_states, key_states, value_states],
        [SLOT_SPEC, frame_spec(0), frame_spec(0), frame_spec(1), frame_spec(1)],
        (wide, wide, wide), 4,
    )
    acc, l = stage(
        near_kernel, info, heads,
        [query_states, near_k, near_v, near_k, near_v, m, acc, l],
        [SLOT_SPEC, frame_spec(0), frame_spec(0), frame_spec(1), frame_spec(1)] + [SLOT_SPEC] * 3,
        (wide, wide), 4,
    )
    attended = stage(
        final_kernel, info, heads,
        [query_states, sink_a, sink_b, far, far, relay, relay, m, acc, l,
         key_states, value_states, near_k, near_v, sink_a, sink_b, far, relay],
        [SLOT_SPEC, frame_spec(0), frame_spec(0), frame_spec(0), frame_spec(1),
         frame_spec(0), frame_spec(1)] + [SLOT_SPEC] * 3 + [HBM_SPEC] * 8,
        jax.ShapeDtypeStruct((rows, width), jnp.bfloat16), 3,
        [pltpu.VMEM((FT, HD), jnp.float32)] * 3
        + [pltpu.VMEM((FT, HD), jnp.bfloat16)] * 2
        + [pltpu.SemaphoreType.DMA((2,))],
    )
    token_rows = lax.all_to_all(attended, "head", split_axis=0, concat_axis=1, tiled=True)
    return jnp.dot(token_rows, out_weight, preferred_element_type=jnp.float32).astype(jnp.bfloat16)


def solution(mesh):
    in_specs = (P("tm", "head"), P("tm", "head"), P("tm", "head"), P("tm"), P("tm"), P())
    out_specs = P(("tm", "head"), None)
    return jax.shard_map(local, mesh=mesh, in_specs=in_specs, out_specs=out_specs, check_vma=False)
```

time: 496 us -> 301 us (0.61)
  the two profiles are of different devices: /device:TPU:18 before, /device:TPU:2 now
where the time goes in v1:
time: 301 us; the launch traced here: 299 us
  Pallas kernels  193 us (64%)
  waiting for transfers between devices  46.4 us (15%)
  starting transfers between devices  17.3 us (6%)
  blocking collectives  16.2 us (5%)
  other arithmetic  12.1 us (4%)
  local copies, waits for them, and re-layouts  9.18 us (3%)
  matrix products  3.95 us (1%)
    pallas_call x3, Pallas kernels, stage(): pl.pallas_call(kernel, grid_spec=grid_spec, out_shape=out_shape, compiler...  193 us
    ppermute x1, waiting for transfers between devices, local(): near_v = lax.ppermute(value_states, axis, onward)  27.1 us
    ppermute x1, waiting for transfers between devices, local(): near_k = lax.ppermute(key_states, axis, onward)  19.3 us
    all_to_all x1, blocking collectives, local(): lax.all_to_all(attended, 'head', split_axis=0, concat_axis=1, tiled=True)  16.2 us
  transfers between devices with their start and end apart: 9, of which 2 were waited for; matrix products, arithmetic and copies ran while one was open for 4% of the time, Pallas kernels for 13%

profile of v1, /device:TPU:2, one launch (start us, length us, event | category | flops | bytes accessed | tf_op | source)
XLA Modules:
  0.0 298.7 jit_solution(13985289988452803841)
XLA Ops:
  0.0 2.8 fusion.1
  2.8 1.5 collective-permute-start
  4.3 2.6 fusion
  7.0 1.7 collective-permute-start.1
  8.6 1.9 collective-permute-start.6
  10.6 3.6 %collective-permute-start.7 = (bf16[1536,512]{1,0:T(8,128)(2,1)}, bf16[1536,512]{1,0:T(8,128)(2,1)}, u32[]{:S(2)}, u32[]{:S(2)}) collective-permute-start(bf16[1536,512]{1,0:T(8,128)(2,1)} %value_hbm.1), channel_id=1, source_target_pairs={{0,2},{2,4},{4,6},{6,8},{8,10},{10,12},{12,14},{14,16},{16,18},{18... | collective-permute-start | bytes 4718600 | tf_op jit(solution)/shard_map/ppermute | solution.py:255
  14.1 2.1 broadcast_select_fusion
  16.3 1.5 collective-permute-start.2
  17.9 2.6 pad_maximum_fusion
  20.5 3.2 %collective-permute-start.5 = (bf16[1536,512]{1,0:T(8,128)(2,1)}, bf16[1536,512]{1,0:T(8,128)(2,1)}, u32[]{:S(2)}, u32[]{:S(2)}) collective-permute-start(bf16[1536,512]{1,0:T(8,128)(2,1)} %pad_maximum_fusion), channel_id=1, source_target_pairs={{0,4},{4,8},{8,12},{12,16},{16,20},{20,24},{24,28},{1,5},{5,9},{9,... | collective-permute-start | bytes 4718600 | tf_op jit(solution)/shard_map/ppermute | solution.py:257
  23.7 19.3 %collective-permute-done.6.k0.k1.near_k_hbm = bf16[1536,512]{1,0:T(8,128)(2,1)} collective-permute-done((bf16[1536,512]{1,0:T(8,128)(2,1)}, bf16[1536,512]{1,0:T(8,128)(2,1)}, u32[]{:S(2)}, u32[]{:S(2)}) %collective-permute-start.6) | collective-permute-done | bytes 1572896 | tf_op jit(solution)/shard_map/ppermute | solution.py:254
  43.0 1.2 slice.24
  44.2 27.1 %collective-permute-done.7.v0.v1.near_v_hbm = bf16[1536,512]{1,0:T(8,128)(2,1)} collective-permute-done((bf16[1536,512]{1,0:T(8,128)(2,1)}, bf16[1536,512]{1,0:T(8,128)(2,1)}, u32[]{:S(2)}, u32[]{:S(2)}) %collective-permute-start.7) | collective-permute-done | bytes 1572896 | tf_op jit(solution)/shard_map/ppermute | solution.py:255
  72.4 1.3 pad_maximum_fusion.1
  73.7 2.6 collective-permute-start.8
  76.3 2.1 broadcast_select_fusion.1
  78.4 1.3 collective-permute-start.3
  79.7 20.4 %shard_map.64 = (f32[1536,512]{1,0:T(8,128)}, f32[1536,512]{1,0:T(8,128)}, f32[1536,512]{1,0:T(8,128)}) custom-call(s32[7]{0:T(128)S(1)} %concatenate.9.info, bf16[1536,512]{1,0:T(8,128)(2,1)S(1)} %copy-done.2, bf16[1536,512]{1,0:T(8,128)(2,1)} %key_hbm.1, bf16[1536,512]{1,0:T(8,128)(2,1)} %value_hbm.1, bf16[1536,512]{1,0:T(8,128)(2,1)} %key_hbm.1, ...), custom_call_target="tpu_custom_call" | custom-call | flops 9663676416 | bytes 16000000 | tf_op jit(solution)/shard_map/pallas_call | solution.py:201
  100.1 1.3 broadcast_select_fusion.2.sink_a.sink_a_hbm
  101.7 17.8 %shard_map.65 = (f32[1536,512]{1,0:T(8,128)}, f32[1536,512]{1,0:T(8,128)}) custom-call(s32[7]{0:T(128)S(1)} %concatenate.9.info, bf16[1536,512]{1,0:T(8,128)(2,1)S(1)} %copy-done.3, bf16[1536,512]{1,0:T(8,128)(2,1)} %collective-permute-done.6.k0.k1.near_k_hbm, bf16[1536,512]{1,0:T(8,128)(2,1)} %collective-permute-done.7.v0.v1.near_v_hbm, ...), custom_call_target="tpu_custom_call" | custom-call | flops 9663676416 | bytes 16000000 | tf_op jit(solution)/shard_map/pallas_call | solution.py:201
  119.6 155.2 %shard_map.66 = bf16[1536,512]{1,0:T(8,128)(2,1)S(1)} custom-call(s32[7]{0:T(128)S(1)} %concatenate.9.info, bf16[1536,512]{1,0:T(8,128)(2,1)S(1)} %copy-done.3, bf16[768,512]{1,0:T(8,128)(2,1)S(1)} %broadcast_select_fusion.2.sink_a.sink_a_hbm, bf16[768,512]{1,0:T(8,128)(2,1)S(1)} %collective-permute-done.4.sink_b.sink_b_hbm, ...), custom_call_target="tpu_custom_call" | custom-call | flops 7247757312 | bytes 16000000 | tf_op jit(solution)/shard_map/pallas_call | solution.py:201
  275.9 2.6 copy.7
  278.5 16.2 %all_to_all.19 = bf16[2,768,512]{1,2,0:T(8,128)(2,1)S(1)} all-to-all(bf16[2,768,512]{1,2,0:T(8,128)(2,1)} %copy.7), channel_id=1, replica_groups=mesh['tm'=16,'head'=2] {'head'}, dimensions={0} | all-to-all | bytes 3145728 | tf_op jit(solution)/shard_map/all_to_all | solution.py:286
  294.7 3.9 %convolution_convert_fusion = bf16[768,1536]{1,0:T(8,128)(2,1)} fusion(bf16[768,1024]{0,1:T(8,128)(2,1)S(1)} %bitcast.10, bf16[1024,1536]{1,0:T(8,128)(2,1)S(1)} %copy-done), kind=kOutput, calls=%fused_computation | convolution fusion | flops 2417098752 | bytes 7077888 | tf_op jit(solution)/shard_map/dot_general | solution.py:287
  (22 shorter events, 2.7 us)
Async XLA Ops:
  0.0 294.7 %copy-start = (bf16[1024,1536]{1,0:T(8,128)(2,1)S(1)}, bf16[1024,1536]{1,0:T(8,128)(2,1)}, u32[]{:S(2)}) copy-start(bf16[1024,1536]{1,0:T(8,128)(2,1)} %param.11) | copy-start | bytes 9437188
  2.8 1.5 collective-permute-start
  7.0 10.9 %copy-start.4 = (s32[2]{0:T(128)S(1)}, s32[2]{0:T(128)}, u32[]{:S(2)}) copy-start(s32[2]{0:T(128)} %param.9) | copy-start | bytes 28
  7.0 10.9 %copy-start.5 = (s32[2]{0:T(128)S(1)}, s32[2]{0:T(128)}, u32[]{:S(2)}) copy-start(s32[2]{0:T(128)} %param.10) | copy-start | bytes 28
  7.0 7.2 %collective-permute-start.1 = (bf16[768,512]{1,0:T(8,128)(2,1)}, bf16[768,512]{1,0:T(8,128)(2,1)}, u32[]{:S(2)}, u32[]{:S(2)}) collective-permute-start(bf16[768,512]{1,0:T(8,128)(2,1)} %get-tuple-element.16), channel_id=1, source_target_pairs={{0,16},{2,6},{1,17},{3,7}} | collective-permute-start | bytes 2359304 | tf_op jit(solution)/shard_map/ppermute | solution.py:228
  8.6 34.3 %collective-permute-start.6 = (bf16[1536,512]{1,0:T(8,128)(2,1)}, bf16[1536,512]{1,0:T(8,128)(2,1)}, u32[]{:S(2)}, u32[]{:S(2)}) collective-permute-start(bf16[1536,512]{1,0:T(8,128)(2,1)} %key_hbm.1), channel_id=1, source_target_pairs={{0,2},{2,4},{4,6},{6,8},{8,10},{10,12},{12,14},{14,16},{16,18},{18... | collective-permute-start | bytes 4718600 | tf_op jit(solution)/shard_map/ppermute | solution.py:254
  10.6 60.7 %collective-permute-start.7 = (bf16[1536,512]{1,0:T(8,128)(2,1)}, bf16[1536,512]{1,0:T(8,128)(2,1)}, u32[]{:S(2)}, u32[]{:S(2)}) collective-permute-start(bf16[1536,512]{1,0:T(8,128)(2,1)} %value_hbm.1), channel_id=1, source_target_pairs={{0,2},{2,4},{4,6},{6,8},{8,10},{10,12},{12,14},{14,16},{16,18},{18... | collective-permute-start | bytes 4718600 | tf_op jit(solution)/shard_map/ppermute | solution.py:255
  16.3 60.0 %collective-permute-start.2 = (bf16[768,512]{1,0:T(8,128)(2,1)}, bf16[768,512]{1,0:T(8,128)(2,1)}, u32[]{:S(2)}, u32[]{:S(2)}) collective-permute-start(bf16[768,512]{1,0:T(8,128)(2,1)} %broadcast_select_fusion), channel_id=1, source_target_pairs={{0,8},{16,24},{2,18},{6,22},{1,9},{17,25},{3,19},{7,23}} | collective-permute-start | bytes 2359304 | tf_op jit(solution)/shard_map/ppermute | solution.py:228
  20.5 99.0 %collective-permute-start.5 = (bf16[1536,512]{1,0:T(8,128)(2,1)}, bf16[1536,512]{1,0:T(8,128)(2,1)}, u32[]{:S(2)}, u32[]{:S(2)}) collective-permute-start(bf16[1536,512]{1,0:T(8,128)(2,1)} %pad_maximum_fusion), channel_id=1, source_target_pairs={{0,4},{4,8},{8,12},{12,16},{16,20},{20,24},{24,28},{1,5},{5,9},{9,... | collective-permute-start | bytes 4718600 | tf_op jit(solution)/shard_map/ppermute | solution.py:257
  73.7 6.0 %copy-start.2 = (bf16[1536,512]{1,0:T(8,128)(2,1)S(1)}, bf16[1536,512]{1,0:T(8,128)(2,1)}, u32[]{:S(2)}) copy-start(bf16[1536,512]{1,0:T(8,128)(2,1)} %q.5) | copy-start | bytes 4718596
  73.7 45.9 %collective-permute-start.8 = (bf16[1536,512]{1,0:T(8,128)(2,1)}, bf16[1536,512]{1,0:T(8,128)(2,1)}, u32[]{:S(2)}, u32[]{:S(2)}) collective-permute-start(bf16[1536,512]{1,0:T(8,128)(2,1)} %pad_maximum_fusion.1), channel_id=1, source_target_pairs={{0,2},{4,6},{8,10},{12,14},{16,18},{20,22},{24,26},{28,30},{1,3},{... | collective-permute-start | bytes 4718600 | tf_op jit(solution)/shard_map/ppermute | solution.py:259
  78.4 21.7 %collective-permute-start.3 = (bf16[768,512]{1,0:T(8,128)(2,1)}, bf16[768,512]{1,0:T(8,128)(2,1)}, u32[]{:S(2)}, u32[]{:S(2)}) collective-permute-start(bf16[768,512]{1,0:T(8,128)(2,1)} %broadcast_select_fusion.1), channel_id=1, source_target_pairs={{0,4},{8,12},{16,20},{24,28},{2,10},{6,14},{18,26},{22,30},{1,5},{... | collective-permute-start | bytes 2359304 | tf_op jit(solution)/shard_map/ppermute | solution.py:228
  100.1 1.6 copy-start.3
  101.4 18.2 %collective-permute-start.4 = (bf16[768,512]{1,0:T(8,128)(2,1)S(1)}, bf16[768,512]{1,0:T(8,128)(2,1)S(1)}, u32[]{:S(2)}, u32[]{:S(2)}) collective-permute-start(bf16[768,512]{1,0:T(8,128)(2,1)S(1)} %broadcast_select_fusion.2.sink_a.sink_a_hbm), channel_id=1, source_target_pairs={{0,2},{2,0},{4,6},{6,4},{8,10},{10,8},{12,14},{14,12},{16,18},{18,... | collective-permute-start | bytes 2359304 | tf_op jit(solution)/shard_map/ppermute | solution.py:233
  274.8 1.1 copy-start.1

commit v2 on v0

v2 whole, which is shorter than its diff:
```python
import jax
import jax.numpy as jnp
from jax import lax
from jax.experimental import pallas as pl
from jax.experimental.pallas import tpu as pltpu
from jax.sharding import PartitionSpec as P

HD = 128
FT = 768
BK = 256
LOG2E = 1.4426950408889634
SCALE = HD ** -0.5 * LOG2E
LIMIT = 1e30
HIDDEN = 1e30
PARAMS = pltpu.CompilerParams(vmem_limit_bytes=28 * 1024 * 1024)
ANY_SPEC = pl.BlockSpec(memory_space=pl.ANY)
COST = pl.CostEstimate(flops=1000, bytes_accessed=1000, transcendentals=0)
TOKEN = jax.ShapeDtypeStruct((8, 128), jnp.float32)
TOKEN_SPEC = pl.BlockSpec((8, 128), lambda *_: (0, 0))


def dot(a, b):
    return jnp.dot(a, b, preferred_element_type=jnp.float32)


def scores(q, kt, unit):
    frame, j = unit
    return dot(q[...], kt[frame, :, j * BK : (j + 1) * BK])


def blocks(*frames):
    return [(frame, j) for frame in frames for j in range(FT // BK)]


def accumulate(units, q, kt, values, shift, old, new, known=None):
    ahead = scores(q, kt, units[0]) if known is None else known
    for n, (frame, j) in enumerate(units):
        s = ahead
        if n + 1 < len(units):
            ahead = scores(q, kt, units[n + 1])
        row_shift = shift[frame]
        parts = [
            jnp.exp2(s[:, c : c + 128] * SCALE - row_shift) for c in range(0, BK, 128)
        ]
        weights = jnp.concatenate([part.astype(jnp.bfloat16) for part in parts], axis=1)
        added = dot(weights, values[frame][j * BK : (j + 1) * BK, :])
        acc_from, l_from = old if n == 0 else new
        if acc_from is None:
            new[0][...] = added
            new[1][...] = sum(parts[1:], parts[0])
        else:
            new[0][...] = acc_from[...] + added
            new[1][...] = sum(parts, l_from[...])


def visible(info, slot, frame):
    return (frame >= 1) & (frame >= info[2 + slot]) & (frame <= info[4 + slot])


def set_shift(shift, frame, seen, m):
    shift[frame] = jnp.where(seen, m[...].astype(jnp.float32), HIDDEN)


def transposed(slot, kt, keys):
    @pl.when(slot == 0)
    def _():
        for frame, k in enumerate(keys):
            kt[frame] = k[...].T


def local_kernel(info, q, k0, k1, v0, v1, m, acc, l, token, kt, shift):
    slot = pl.program_id(1)
    first = info[0]
    token[...] = jnp.zeros_like(token)
    transposed(slot, kt, (k0, k1))

    def run(own):
        known = scores(q, kt, (own, 0))
        peak = jnp.max(known, axis=1, keepdims=True) * SCALE
        m[...] = jnp.broadcast_to(peak, (FT, HD)).astype(m.dtype)
        for frame in (0, 1):
            set_shift(shift, frame, visible(info, own, first + frame), m)
        units = blocks(own, 1 - own)
        accumulate(units, q, kt, (v0, v1), shift, (None, None), (acc, l), known)

    pl.when(slot == 0)(lambda: run(0))
    pl.when(slot == 1)(lambda: run(1))


def near_kernel(info, q, k0, k1, v0, v1, m, acc_in, l_in, acc, l, kt, shift):
    slot = pl.program_id(1)
    first = info[0]
    transposed(slot, kt, (k0, k1))
    for frame in (0, 1):
        set_shift(shift, frame, visible(info, slot, first - 2 + frame), m)
    accumulate(blocks(1, 0), q, kt, (v0, v1), shift, (acc_in, l_in), (acc, l))


def final_kernel(
    offset, info, q, sink_a, sink_b, far_k, far_v, relay_k, relay_v, m, acc_in, l_in,
    key_hbm, value_hbm, near_k, near_v, sink_a_hbm, sink_b_hbm, far, relay, *refs,
):
    outs = refs[:-7]
    acc, l, sem, kt, shift, values, k_buf = refs[-7:]
    head = pl.program_id(0) + offset
    slot = pl.program_id(1)
    first = info[0]
    core = info[6]

    @pl.when(slot == 0)
    def _():
        for here, listed in (
            (0, (sink_a, sink_b, far_k, far_v)),
            (1, (sink_b, sink_a, relay_k, relay_v)),
        ):

            @pl.when(core == here)
            def _():
                for frame in (0, 1):
                    kt[frame] = listed[2 * frame][...].T
                    values[frame] = listed[2 * frame + 1][...]

    far_seen = (slot == 0) & visible(info, slot, first - 3)
    set_shift(shift, 0, True, m)

    @pl.when(slot == 0)
    def _():
        set_shift(shift, 1, far_seen, m)
        accumulate(blocks(0, 1), q, kt, values, shift, (acc_in, l_in), (acc, l))

    @pl.when(slot == 1)
    def _():
        accumulate(blocks(0), q, kt, values, shift, (acc_in, l_in), (acc, l))

    def write():
        total = jnp.sum(l[...], axis=1, keepdims=True)
        attended = (acc[...] / total).astype(jnp.bfloat16)
        if len(outs) == 1:
            outs[0][pl.ds(pl.multiple_of(slot * FT, FT), FT), :] = attended
        else:

            @pl.when(info[1] == slot)
            def _():
                outs[0][...] = attended

            @pl.when(info[1] != slot)
            def _():
                outs[1][...] = attended

        return jnp.max(total)

    in_range = write() < LIMIT

    @pl.when(jnp.logical_not(in_range))
    def _():
        columns = pl.ds(pl.multiple_of(head * HD, HD), HD)
        sources = [
            (core == 0, sink_a_hbm, 0, sink_b_hbm, 0),
            (core == 1, sink_b_hbm, 0, sink_a_hbm, 0),
            (far_seen & (core == 0), far, 0, far, FT),
            (far_seen & (core == 1), relay, 0, relay, FT),
        ]
        for frame in (0, 1):
            row = frame * FT
            own = visible(info, slot, first + frame)
            sources.append((own, key_hbm, row, value_hbm, row))
            behind = visible(info, slot, first - 2 + frame)
            sources.append((behind, near_k, row, near_v, row))

        def sweep(step):
            def turn(t, carry):
                seen = False
                for i, (shown, k_hbm, k_row, v_hbm, v_row) in enumerate(sources):
                    chosen = (t == i) & shown
                    seen = seen | chosen

                    @pl.when(chosen)
                    def _():
                        pairs = ((k_hbm, k_row, k_buf), (v_hbm, v_row, values.at[0]))
                        for n, (hbm, row, buf) in enumerate(pairs):
                            copy = pltpu.make_async_copy(
                                hbm.at[pl.ds(row, FT), columns], buf, sem.at[n]
                            )
                            copy.start()
                            copy.wait()

                @pl.when(seen)
                def _():
                    kt[0] = k_buf[...].T
                    step()

                return carry

            lax.fori_loop(0, len(sources), turn, 0)

        def peak():
            for unit in blocks(0):
                here = jnp.max(scores(q, kt, unit), axis=1, keepdims=True) * SCALE
                shift[0] = jnp.maximum(shift[0], here)

        shift[0] = jnp.full((FT, HD), -jnp.inf, jnp.float32)
        acc[...] = jnp.zeros((FT, HD), jnp.float32)
        l[...] = jnp.zeros((FT, HD), jnp.float32)
        sweep(peak)
        sweep(lambda: accumulate(blocks(0), q, kt, values, shift, (acc, l), (acc, l)))
        write()

        @pl.when(slot == 0)
        def _():
            for here, (k, v) in ((0, (sink_a, sink_b)), (1, (sink_b, sink_a))):

                @pl.when(core == here)
                def _():
                    kt[0] = k[...].T
                    values[0] = v[...]


SLOT = "slot"


def stage(kernel, info, group, arrays, specs, outs, scratch=(), token=False):
    offset, heads = group

    def spec(entry):
        if entry is None:
            return ANY_SPEC
        block, whole = entry
        base = offset if whole else 0
        if block == SLOT:
            return pl.BlockSpec((FT, HD), lambda h, s, info: (s, h + base))
        return pl.BlockSpec((FT, HD), lambda h, s, info: (block, h + base))

    out_specs, shapes = [], []
    for rows, dtype, block in outs:
        shapes.append(jax.ShapeDtypeStruct((rows, heads * HD), dtype))
        if block is None:
            out_specs.append(pl.BlockSpec((rows, HD), lambda h, s, info: (0, h)))
        else:
            out_specs.append(spec((block, False)))
    return pl.pallas_call(
        kernel,
        grid_spec=pltpu.PrefetchScalarGridSpec(
            num_scalar_prefetch=1,
            grid=(heads, 2),
            in_specs=[spec(entry) for entry in specs],
            out_specs=out_specs + [TOKEN_SPEC] * token,
            scratch_shapes=list(scratch)
            + [
                pltpu.VMEM((2, HD, FT), jnp.bfloat16),
                pltpu.VMEM((2, FT, HD), jnp.float32),
            ]
            + ([pltpu.VMEM((2, FT, HD), jnp.bfloat16), pltpu.VMEM((FT, HD), jnp.bfloat16)]
               if scratch else []),
        ),
        out_shape=shapes + [TOKEN] * token,
        compiler_params=PARAMS,
        cost_estimate=COST,
    )(info, *arrays)


def pick(flag, taken, kept, tokens=()):
    flag = jnp.reshape(flag, (1,)).astype(jnp.int32)
    rows, width = taken.shape
    turns = 3
    block = rows // turns

    def kernel(flag, taken, kept, *refs):
        out = refs[-1]

        @pl.when(flag[0] == 1)
        def _():
            out[...] = taken[...]

        @pl.when(flag[0] == 0)
        def _():
            out[...] = kept[...]

    def spec(index):
        return pl.BlockSpec((block, width), index)

    return pl.pallas_call(
        kernel,
        grid_spec=pltpu.PrefetchScalarGridSpec(
            num_scalar_prefetch=1,
            grid=(turns,),
            in_specs=[
                spec(lambda i, flag: (i * flag[0], 0)), spec(lambda i, flag: (i - i * flag[0], 0))
            ] + [TOKEN_SPEC] * len(tokens),
            out_specs=spec(lambda i, flag: (i, 0)),
        ),
        out_shape=jax.ShapeDtypeStruct((rows, width), taken.dtype),
        compiler_params=PARAMS,
        cost_estimate=COST,
    )(flag, taken, kept, *tokens)


def last_frames(keys, values):
    width = keys.shape[1]
    turns = 4
    block = 2 * FT // turns

    def kernel(keys, values, out):
        i = pl.program_id(0)

        @pl.when(i < turns // 2)
        def _():
            out[...] = keys[...]

        @pl.when(i >= turns // 2)
        def _():
            out[...] = values[...]

    def spec(index):
        return pl.BlockSpec((block, width), index)

    half = turns // 2
    return pl.pallas_call(
        kernel,
        grid=(turns,),
        in_specs=[
            spec(lambda i: (half + jnp.minimum(i, half - 1), 0)),
            spec(lambda i: (jnp.maximum(i, half), 0)),
        ],
        out_specs=spec(lambda i: (i, 0)),
        out_shape=jax.ShapeDtypeStruct((2 * FT, width), keys.dtype),
        compiler_params=PARAMS,
        cost_estimate=COST,
    )(keys, values)


def sink_steps(size):
    bits = [1 << b for b in range(1, size.bit_length() - 1)]
    orders = (bits[::-1], [bits[0]] + bits[:0:-1])
    done = [0, 0]
    steps = []
    for step in range(len(bits)):
        pairs = []
        for which in (0, 1):
            bit = orders[which][step]
            holders = [i for i in range(0, size, 2) if i & ~done[which] == 0]
            pairs += [(i + which, (i | bit) + which) for i in holders]
            done[which] |= bit
        steps.append(pairs)
    return steps


def project(info, parts, weight):
    columns = weight.shape[1]
    turns = 6
    block = columns // turns
    rows, depth = parts[0][0].shape
    per_device = weight.shape[0] // 2 // depth
    n = len(parts)

    def kernel(info, *refs):
        products = [dot(a[...], w[...]) for a, w in zip(refs[:n], refs[n : 2 * n])]
        refs[-1][...] = sum(products[1:], products[0]).astype(jnp.bfloat16)

    def weight_spec(part, received):
        def index(i, info):
            owner = 1 - info[1] if received else info[1]
            return (owner * per_device + part, i)

        return pl.BlockSpec((depth, block), index)

    return pl.pallas_call(
        kernel,
        grid_spec=pltpu.PrefetchScalarGridSpec(
            num_scalar_prefetch=1,
            grid=(turns,),
            in_specs=[pl.BlockSpec((rows, depth), lambda i, info: (0, 0))] * n
            + [weight_spec(part, received) for _, part, received in parts],
            out_specs=pl.BlockSpec((rows, block), lambda i, info: (0, i)),
        ),
        out_shape=jax.ShapeDtypeStruct((rows, columns), jnp.bfloat16),
        compiler_params=PARAMS,
        cost_estimate=COST,
    )(info, *[a for a, _, _ in parts], *[weight] * n)


def local(query_states, key_states, value_states, win_start, group_end, out_weight):
    axis = "tm"
    size = lax.axis_size(axis)
    paired = lax.axis_size("head") == 2
    me = lax.axis_index(axis)
    core = me % 2
    heads = query_states.shape[1] // HD
    info = jnp.concatenate(
        [
            jnp.stack([me * 2, lax.axis_index("head")]).astype(jnp.int32),
            win_start.astype(jnp.int32),
            group_end.astype(jnp.int32),
            jnp.stack([core]).astype(jnp.int32),
        ]
    )
    groups = [(0, heads // 2), (heads // 2, heads // 2)] if heads % 2 == 0 else [(0, heads)]
    slot_all, slot_part = (SLOT, True), (SLOT, False)
    frames = [(0, True), (1, True)]
    sums = [(2 * FT, jnp.float32, SLOT)] * 2

    onward = [(i, i + 1) for i in range(size - 1)]
    near_k = lax.ppermute(key_states, axis, onward)
    near_v = lax.ppermute(value_states, axis, onward)

    def local_stage(group):
        return stage(
            local_kernel, info, group,
            [query_states, key_states, key_states, value_states, value_states],
            [slot_all] + frames * 2, [(2 * FT, jnp.bfloat16, SLOT)] + sums, token=True,
        )

    moved = lax.ppermute(value_states[:FT], axis, [(0, 1)])
    held = pick(core, moved, key_states[:FT])
    states = []
    for step, pairs in enumerate(sink_steps(size)):
        moved = lax.ppermute(held, axis, pairs)
        tokens = []
        if step < len(groups):
            *state, token = local_stage(groups[step])
            states.append(state)
            tokens = [token]
        takes = jnp.zeros((), bool)
        for _, target in pairs:
            takes = takes | (me == target)
        held = pick(takes, moved, held, tokens)
    other = lax.ppermute(held, axis, [(i, i ^ 1) for i in range(size)])

    own_last = last_frames(key_states, value_states)
    far = lax.ppermute(own_last, axis, [(i, i + 2) for i in range(0, size - 2, 2)])
    near_last = last_frames(near_k, near_v)
    relay = lax.ppermute(near_last, axis, [(i, i + 1) for i in range(0, size, 2)])

    for g, group in enumerate(groups):
        m, acc, l = states[g]
        acc, l = stage(
            near_kernel, info, group, [query_states, near_k, near_k, near_v, near_v, m, acc, l],
            [slot_all] + frames * 2 + [slot_part] * 3, sums,
        )
        states[g] = m, acc, l
    mine, theirs = [], []
    for g, group in enumerate(groups):
        outs = [(FT, jnp.bfloat16, 0)] * 2 if paired else [(2 * FT, jnp.bfloat16, None)]
        results = stage(
            lambda *refs, offset=group[0]: final_kernel(offset, *refs), info, group,
            [query_states, held, other, far, far, relay, relay, *states[g],
             key_states, value_states, near_k, near_v, held, other, far, relay],
            [slot_all, frames[0], frames[0]] + frames * 2 + [slot_part] * 3 + [None] * 8, outs,
            [pltpu.VMEM((FT, HD), jnp.float32)] * 2 + [pltpu.SemaphoreType.DMA((2,))],
        )
        mine.append(results[0])
        if paired:
            theirs.append(lax.ppermute(results[1], "head", [(0, 1), (1, 0)]))
    if not paired:
        attended = jnp.concatenate(mine, axis=1)
        token_rows = lax.all_to_all(attended, "head", split_axis=0, concat_axis=1, tiled=True)
        return dot(token_rows, out_weight).astype(jnp.bfloat16)
    parts = [(array, g, False) for g, array in enumerate(mine)]
    parts += [(array, g, True) for g, array in enumerate(theirs)]
    return project(info, parts, out_weight)


def solution(mesh):
    in_specs = (P("tm", "head"), P("tm", "head"), P("tm", "head"), P("tm"), P("tm"), P())
    out_specs = P(("tm", "head"), None)
    return jax.shard_map(local, mesh=mesh, in_specs=in_specs, out_specs=out_specs, check_vma=False)
```

time: 496 us -> 298 us (0.60)
  the two profiles are of different devices: /device:TPU:18 before, /device:TPU:10 now
where the time goes in v2:
time: 298 us; the launch traced here: 299 us
  Pallas kernels  230 us (77%)
  starting transfers between devices  35.4 us (12%)
  waiting for transfers between devices  17.8 us (6%)
  local copies, waits for them, and re-layouts  15.2 us (5%)
    pallas_call x6, Pallas kernels, stage(): pl.pallas_call(kernel, grid_spec=pltpu.PrefetchScalarGridSpec(num_scalar_...  209 us
    ppermute x1, starting transfers between devices, local(): other = lax.ppermute(held, axis, [(i, i ^ 1) for i in range(size)])  13.1 us
    unnamed x42, local copies, waits for them, and re-layouts  12 us
    ppermute x3, waiting for transfers between devices, local(): moved = lax.ppermute(held, axis, pairs)  10.5 us
    pallas_call x4, Pallas kernels, pick(): pl.pallas_call(kernel, grid_spec=pltpu.PrefetchScalarGridSpec(num_scalar_...  10.4 us
    ppermute x2, waiting for transfers between devices, local(): theirs.append(lax.ppermute(results[1], 'head', [(0, 1), (1, 0)]))  7.29 us
    ppermute x1, starting transfers between devices, local(): lax.ppermute(own_last, axis, [(i, i + 2) for i in range(0, size - 2, 2)])  6.45 us
  transfers between devices with their start and end apart: 11, of which 2 were waited for; matrix products, arithmetic and copies ran while one was open for 0% of the time, Pallas kernels for 45%

profile of v2, /device:TPU:10, one launch (start us, length us, event | category | flops | bytes accessed | tf_op | source)
XLA Modules:
  0.0 298.6 jit_solution(5629975304607236535)
XLA Ops:
  0.0 2.2 slice.6
  6.0 2.4 shard_map.64.kept
  8.3 1.5 collective-permute-start.1
  9.9 2.2 collective-permute-start.6
  12.1 3.0 %collective-permute-start.7 = (bf16[1536,512]{1,0:T(8,128)(2,1)S(1)}, bf16[1536,512]{1,0:T(8,128)(2,1)}, u32[]{:S(2)}, u32[]{:S(2)}) collective-permute-start(bf16[1536,512]{1,0:T(8,128)(2,1)S(1)} %copy-done), channel_id=1, source_target_pairs={{0,2},{2,4},{4,6},{6,8},{8,10},{10,12},{12,14},{14,16},{16,18},{18... | collective-permute-start | bytes 4718600 | tf_op jit(solution)/shard_map/ppermute | solution.py:403
  16.7 8.4 %shard_map.65 = (bf16[1536,256]{1,0:T(8,128)(2,1)S(1)}, f32[1536,256]{1,0:T(8,128)S(1)}, f32[1536,256]{1,0:T(8,128)S(1)}, f32[8,128]{1,0:T(8,128)S(1)}) custom-call(s32[7]{0:T(128)S(1)} %concatenate.3.info.refs_0_, bf16[1536,512]{1,0:T(8,128)(2,1)S(1)} %copy-done.2, bf16[1536,512]{1,0:T(8,128)(2,1)S(1)} %copy-done.1, bf16[1536,512]{1,0:T(8,128)(2,1)S(1)} %copy-done.1, ...), custom_call_target="tpu_custom_call" | custom-call | flops 1000 | bytes 1000 | tf_op jit(solution)/shard_map/pallas_call | solution.py:240
  28.3 3.0 shard_map.66.kept
  31.3 1.7 collective-permute-start.2
  32.9 1.7 shard_map.70
  34.6 6.5 %collective-permute-start.5 = (bf16[1536,512]{1,0:T(8,128)(2,1)}, bf16[1536,512]{1,0:T(8,128)(2,1)}, u32[]{:S(2)}, u32[]{:S(2)}) collective-permute-start(bf16[1536,512]{1,0:T(8,128)(2,1)} %shard_map.70), channel_id=1, source_target_pairs={{0,4},{4,8},{8,12},{12,16},{16,20},{20,24},{24,28},{1,5},{5,9},{9,... | collective-permute-start | bytes 4718600 | tf_op jit(solution)/shard_map/ppermute | solution.py:429
  41.1 8.4 %shard_map.67 = (bf16[1536,256]{1,0:T(8,128)(2,1)S(1)}, f32[1536,256]{1,0:T(8,128)S(1)}, f32[1536,256]{1,0:T(8,128)S(1)}, f32[8,128]{1,0:T(8,128)S(1)}) custom-call(s32[7]{0:T(128)S(1)} %concatenate.3.info.refs_0_, bf16[1536,512]{1,0:T(8,128)(2,1)S(1)} %copy-done.3, bf16[1536,512]{1,0:T(8,128)(2,1)S(1)} %copy-done.1, bf16[1536,512]{1,0:T(8,128)(2,1)S(1)} %copy-done.1, ...), custom_call_target="tpu_custom_call" | custom-call | flops 1000 | bytes 1000 | tf_op jit(solution)/shard_map/pallas_call | solution.py:240
  52.7 2.9 shard_map.68.kept
  57.0 3.9 %shard_map.71 = bf16[1536,512]{1,0:T(8,128)(2,1)} custom-call(bf16[1536,512]{1,0:T(8,128)(2,1)} %collective-permute-done.6.keys.k0.k1.refs_13_, bf16[1536,512]{1,0:T(8,128)(2,1)} %collective-permute-done.7.values.v0.v1.refs_14_), custom_call_target="tpu_custom_call" | custom-call | flops 1000 | bytes 1000 | tf_op jit(solution)/shard_map/pallas_call | solution.py:317
  60.8 2.5 collective-permute-start.8
  63.3 10.5 %collective-permute-done.3.taken = bf16[768,512]{1,0:T(8,128)(2,1)} collective-permute-done((bf16[768,512]{1,0:T(8,128)(2,1)}, bf16[768,512]{1,0:T(8,128)(2,1)}, u32[]{:S(2)}, u32[]{:S(2)}) %collective-permute-start.3) | collective-permute-done | bytes 786464 | tf_op jit(solution)/shard_map/ppermute | solution.py:416
  73.8 2.1 shard_map.69.refs_2_.refs_15_
  75.9 13.1 %collective-permute-start.4 = (bf16[768,512]{1,0:T(8,128)(2,1)S(1)}, bf16[768,512]{1,0:T(8,128)(2,1)S(1)}, u32[]{:S(2)}, u32[]{:S(2)}) collective-permute-start(bf16[768,512]{1,0:T(8,128)(2,1)S(1)} %shard_map.69.refs_2_.refs_15_), channel_id=1, source_target_pairs={{0,2},{2,0},{4,6},{6,4},{8,10},{10,8},{12,14},{14,12},{16,18},{18,... | collective-permute-start | bytes 2359304 | tf_op jit(solution)/shard_map/ppermute | solution.py:426
  91.8 9.3 %shard_map.74 = (f32[1536,256]{1,0:T(8,128)S(1)}, f32[1536,256]{1,0:T(8,128)S(1)}) custom-call(s32[7]{0:T(128)S(1)} %concatenate.3.info.refs_0_, bf16[1536,512]{1,0:T(8,128)(2,1)S(1)} %copy-done.4, bf16[1536,512]{1,0:T(8,128)(2,1)} %collective-permute-done.6.keys.k0.k1.refs_13_, bf16[1536,512]{1,0:T(8,128)(2,1)} %collective-permute-done.6.keys.k0.k1.refs_13_, ...), custom_call_target="tpu_custom_call" | custom-call | flops 1000 | bytes 1000 | tf_op jit(solution)/shard_map/pallas_call | solution.py:240
  101.2 9.1 %shard_map.72 = (f32[1536,256]{1,0:T(8,128)S(1)}, f32[1536,256]{1,0:T(8,128)S(1)}) custom-call(s32[7]{0:T(128)S(1)} %concatenate.3.info.refs_0_, bf16[1536,512]{1,0:T(8,128)(2,1)S(1)} %copy-done.4, bf16[1536,512]{1,0:T(8,128)(2,1)} %collective-permute-done.6.keys.k0.k1.refs_13_, bf16[1536,512]{1,0:T(8,128)(2,1)} %collective-permute-done.6.keys.k0.k1.refs_13_, ...), custom_call_target="tpu_custom_call" | custom-call | flops 1000 | bytes 1000 | tf_op jit(solution)/shard_map/pallas_call | solution.py:240
  110.3 86.6 %shard_map.73 = (bf16[768,256]{1,0:T(8,128)(2,1)S(1)}, bf16[768,256]{1,0:T(8,128)(2,1)S(1)}) custom-call(s32[7]{0:T(128)S(1)} %concatenate.3.info.refs_0_, bf16[1536,512]{1,0:T(8,128)(2,1)S(1)} %copy-done.4, bf16[768,512]{1,0:T(8,128)(2,1)S(1)} %shard_map.69.refs_2_.refs_15_, bf16[768,512]{1,0:T(8,128)(2,1)S(1)} %collective-permute-done.4.refs_3_.refs_16_, ...), custom_call_target="tpu_custom_call" | custom-call | flops 1000 | bytes 1000 | tf_op jit(solution)/shard_map/pallas_call | solution.py:240
  196.9 1.6 collective-permute-start.9
  198.5 86.9 %shard_map.75 = (bf16[768,256]{1,0:T(8,128)(2,1)S(1)}, bf16[768,256]{1,0:T(8,128)(2,1)S(1)}) custom-call(s32[7]{0:T(128)S(1)} %concatenate.3.info.refs_0_, bf16[1536,512]{1,0:T(8,128)(2,1)S(1)} %copy-done.4, bf16[768,512]{1,0:T(8,128)(2,1)S(1)} %shard_map.69.refs_2_.refs_15_, bf16[768,512]{1,0:T(8,128)(2,1)S(1)} %collective-permute-done.4.refs_3_.refs_16_, ...), custom_call_target="tpu_custom_call" | custom-call | flops 1000 | bytes 1000 | tf_op jit(solution)/shard_map/pallas_call | solution.py:240
  285.9 7.3 %collective-permute-done.10.refs_3_ = bf16[768,256]{1,0:T(8,128)(2,1)S(1)} collective-permute-done((bf16[768,256]{1,0:T(8,128)(2,1)S(1)}, bf16[768,256]{1,0:T(8,128)(2,1)S(1)}, u32[]{:S(2)}, u32[]{:S(2)}) %collective-permute-start.10) | collective-permute-done | bytes 393248 | tf_op jit(solution)/shard_map/ppermute | solution.py:452
  293.2 5.4 %shard_map.76 = bf16[768,1536]{1,0:T(8,128)(2,1)} custom-call(s32[7]{0:T(128)S(1)} %concatenate.3.info.refs_0_, bf16[768,256]{1,0:T(8,128)(2,1)S(1)} %get-tuple-element.28.refs_0_, bf16[768,256]{1,0:T(8,128)(2,1)S(1)} %get-tuple-element.34.refs_1_, bf16[768,256]{1,0:T(8,128)(2,1)S(1)} %collective-permute-done.9.refs_2_, ...), custom_call_target="tpu_custom_call" | custom-call | flops 1000 | bytes 1000 | tf_op jit(solution)/shard_map/pallas_call | solution.py:366
  (56 shorter events, 16.4 us)
Async XLA Ops:
  0.0 3.7 %copy-start.1 = (bf16[1536,512]{1,0:T(8,128)(2,1)S(1)}, bf16[1536,512]{1,0:T(8,128)(2,1)}, u32[]{:S(2)}) copy-start(bf16[1536,512]{1,0:T(8,128)(2,1)} %refs_11_.3) | copy-start | bytes 4718596
  2.2 2.5 collective-permute-start
  3.7 11.4 %copy-start.19 = (s32[2]{0:T(128)S(1)}, s32[2]{0:T(128)}, u32[]{:S(2)}) copy-start(s32[2]{0:T(128)} %param.9) | copy-start | bytes 28
  3.7 11.4 %copy-start.20 = (s32[2]{0:T(128)S(1)}, s32[2]{0:T(128)}, u32[]{:S(2)}) copy-start(s32[2]{0:T(128)} %param.10) | copy-start | bytes 28
  4.7 7.4 %copy-start = (bf16[1536,512]{1,0:T(8,128)(2,1)S(1)}, bf16[1536,512]{1,0:T(8,128)(2,1)}, u32[]{:S(2)}) copy-start(bf16[1536,512]{1,0:T(8,128)(2,1)} %refs_12_.3) | copy-start | bytes 4718596
  8.3 20.0 %collective-permute-start.1 = (bf16[768,512]{1,0:T(8,128)(2,1)}, bf16[768,512]{1,0:T(8,128)(2,1)}, u32[]{:S(2)}, u32[]{:S(2)}) collective-permute-start(bf16[768,512]{1,0:T(8,128)(2,1)} %shard_map.64.kept), channel_id=1, source_target_pairs={{0,16},{2,6},{1,17},{3,7}} | collective-permute-start | bytes 2359304 | tf_op jit(solution)/shard_map/ppermute | solution.py:416
  9.9 47.1 %collective-permute-start.6 = (bf16[1536,512]{1,0:T(8,128)(2,1)S(1)}, bf16[1536,512]{1,0:T(8,128)(2,1)}, u32[]{:S(2)}, u32[]{:S(2)}) collective-permute-start(bf16[1536,512]{1,0:T(8,128)(2,1)S(1)} %copy-done.1), channel_id=1, source_target_pairs={{0,2},{2,4},{4,6},{6,8},{8,10},{10,12},{12,14},{14,16},{16,18},{18... | collective-permute-start | bytes 4718600 | tf_op jit(solution)/shard_map/ppermute | solution.py:402
  12.1 44.9 %collective-permute-start.7 = (bf16[1536,512]{1,0:T(8,128)(2,1)S(1)}, bf16[1536,512]{1,0:T(8,128)(2,1)}, u32[]{:S(2)}, u32[]{:S(2)}) collective-permute-start(bf16[1536,512]{1,0:T(8,128)(2,1)S(1)} %copy-done), channel_id=1, source_target_pairs={{0,2},{2,4},{4,6},{6,8},{8,10},{10,12},{12,14},{14,16},{16,18},{18... | collective-permute-start | bytes 4718600 | tf_op jit(solution)/shard_map/ppermute | solution.py:403
  15.2 1.4 copy-start.2
  31.3 9.8 %copy-start.3 = (bf16[1536,512]{1,0:T(8,128)(2,1)S(1)}, bf16[1536,512]{1,0:T(8,128)(2,1)}, u32[]{:S(2)}) copy-start(bf16[1536,512]{1,0:T(8,128)(2,1)} %refs_1_.3) | copy-start | bytes 4718596
  31.3 21.5 %collective-permute-start.2 = (bf16[768,512]{1,0:T(8,128)(2,1)}, bf16[768,512]{1,0:T(8,128)(2,1)}, u32[]{:S(2)}, u32[]{:S(2)}) collective-permute-start(bf16[768,512]{1,0:T(8,128)(2,1)} %shard_map.66.kept), channel_id=1, source_target_pairs={{0,8},{16,24},{2,18},{6,22},{1,9},{17,25},{3,19},{7,23}} | collective-permute-start | bytes 2359304 | tf_op jit(solution)/shard_map/ppermute | solution.py:416
  34.6 75.7 %collective-permute-start.5 = (bf16[1536,512]{1,0:T(8,128)(2,1)}, bf16[1536,512]{1,0:T(8,128)(2,1)}, u32[]{:S(2)}, u32[]{:S(2)}) collective-permute-start(bf16[1536,512]{1,0:T(8,128)(2,1)} %shard_map.70), channel_id=1, source_target_pairs={{0,4},{4,8},{8,12},{12,16},{16,20},{20,24},{24,28},{1,5},{5,9},{9,... | collective-permute-start | bytes 4718600 | tf_op jit(solution)/shard_map/ppermute | solution.py:429
  55.7 18.2 %collective-permute-start.3 = (bf16[768,512]{1,0:T(8,128)(2,1)}, bf16[768,512]{1,0:T(8,128)(2,1)}, u32[]{:S(2)}, u32[]{:S(2)}) collective-permute-start(bf16[768,512]{1,0:T(8,128)(2,1)} %shard_map.68.kept), channel_id=1, source_target_pairs={{0,4},{8,12},{16,20},{24,28},{2,10},{6,14},{18,26},{22,30},{1,5},{... | collective-permute-start | bytes 2359304 | tf_op jit(solution)/shard_map/ppermute | solution.py:416
  60.8 49.5 %collective-permute-start.8 = (bf16[1536,512]{1,0:T(8,128)(2,1)}, bf16[1536,512]{1,0:T(8,128)(2,1)}, u32[]{:S(2)}, u32[]{:S(2)}) collective-permute-start(bf16[1536,512]{1,0:T(8,128)(2,1)} %shard_map.71), channel_id=1, source_target_pairs={{0,2},{4,6},{8,10},{12,14},{16,18},{20,22},{24,26},{28,30},{1,3},{... | collective-permute-start | bytes 4718600 | tf_op jit(solution)/shard_map/ppermute | solution.py:431
  63.3 25.7 %copy-start.4 = (bf16[1536,512]{1,0:T(8,128)(2,1)S(1)}, bf16[1536,512]{1,0:T(8,128)(2,1)}, u32[]{:S(2)}) copy-start(bf16[1536,512]{1,0:T(8,128)(2,1)} %refs_1_.3) | copy-start | bytes 4718596
  63.3 25.7 %copy-start.10 = (bf16[1536,256]{1,0:T(8,128)(2,1)S(1)}, bf16[1536,256]{1,0:T(8,128)(2,1)}, u32[]{:S(2)}) copy-start(bf16[1536,256]{1,0:T(8,128)(2,1)} %copy-done.9) | copy-start | bytes 2359300
  75.9 34.4 %collective-permute-start.4 = (bf16[768,512]{1,0:T(8,128)(2,1)S(1)}, bf16[768,512]{1,0:T(8,128)(2,1)S(1)}, u32[]{:S(2)}, u32[]{:S(2)}) collective-permute-start(bf16[768,512]{1,0:T(8,128)(2,1)S(1)} %shard_map.69.refs_2_.refs_15_), channel_id=1, source_target_pairs={{0,2},{2,0},{4,6},{6,4},{8,10},{10,8},{12,14},{14,12},{16,18},{18,... | collective-permute-start | bytes 2359304 | tf_op jit(solution)/shard_map/ppermute | solution.py:426
  89.0 1.4 copy-start.16
  91.8 9.4 %copy-start.8 = (bf16[1536,256]{1,0:T(8,128)(2,1)S(1)}, bf16[1536,256]{1,0:T(8,128)(2,1)}, u32[]{:S(2)}) copy-start(bf16[1536,256]{1,0:T(8,128)(2,1)} %copy-done.7) | copy-start | bytes 2359300
  91.8 9.4 %copy-start.12 = (f32[1536,256]{1,0:T(8,128)S(1)}, f32[1536,256]{1,0:T(8,128)}, u32[]{:S(2)}) copy-start(f32[1536,256]{1,0:T(8,128)} %copy-done.11) | copy-start | bytes 4718596
  91.8 9.4 %copy-start.14 = (f32[1536,256]{1,0:T(8,128)S(1)}, f32[1536,256]{1,0:T(8,128)}, u32[]{:S(2)}) copy-start(f32[1536,256]{1,0:T(8,128)} %copy-done.13) | copy-start | bytes 4718596
  196.9 89.0 %collective-permute-start.9 = (bf16[768,256]{1,0:T(8,128)(2,1)S(1)}, bf16[768,256]{1,0:T(8,128)(2,1)S(1)}, u32[]{:S(2)}, u32[]{:S(2)}) collective-permute-start(bf16[768,256]{1,0:T(8,128)(2,1)S(1)} %get-tuple-element.35), channel_id=1, source_target_pairs={{0,1},{1,0},{2,3},{3,2},{4,5},{5,4},{6,7},{7,6},{8,9},{9,8},{10,11... | collective-permute-start | bytes 1179656 | tf_op jit(solution)/shard_map/ppermute | solution.py:452
  198.5 94.7 %copy-start.5 = (bf16[1024,1536]{1,0:T(8,128)(2,1)S(1)}, bf16[1024,1536]{1,0:T(8,128)(2,1)}, u32[]{:S(2)}) copy-start(bf16[1024,1536]{1,0:T(8,128)(2,1)} %refs_7_.1) | copy-start | bytes 9437188
  285.4 7.8 %collective-permute-start.10 = (bf16[768,256]{1,0:T(8,128)(2,1)S(1)}, bf16[768,256]{1,0:T(8,128)(2,1)S(1)}, u32[]{:S(2)}, u32[]{:S(2)}) collective-permute-start(bf16[768,256]{1,0:T(8,128)(2,1)S(1)} %get-tuple-element.36), channel_id=1, source_target_pairs={{0,1},{1,0},{2,3},{3,2},{4,5},{5,4},{6,7},{7,6},{8,9},{9,8},{10,11... | collective-permute-start | bytes 1179656 | tf_op jit(solution)/shard_map/ppermute | solution.py:452
  (8 other events, 9.1 us)

commit v3 on v2

--- a/solution.py
+++ b/solution.py
@@ -12,7 +12,7 @@
 SCALE = HD ** -0.5 * LOG2E
 LIMIT = 1e30
 HIDDEN = 1e30
-PARAMS = pltpu.CompilerParams(vmem_limit_bytes=28 * 1024 * 1024)
+PARAMS = pltpu.CompilerParams(vmem_limit_bytes=56 * 1024 * 1024)
 ANY_SPEC = pl.BlockSpec(memory_space=pl.ANY)
 COST = pl.CostEstimate(flops=1000, bytes_accessed=1000, transcendentals=0)
 TOKEN = jax.ShapeDtypeStruct((8, 128), jnp.float32)
@@ -87,8 +87,9 @@
     pl.when(slot == 1)(lambda: run(1))
 
 
-def near_kernel(info, q, k0, k1, v0, v1, m, acc_in, l_in, acc, l, kt, shift):
+def near_kernel(info, q, k0, k1, v0, v1, m, acc_in, l_in, acc, l, token, kt, shift):
     slot = pl.program_id(1)
+    token[...] = jnp.zeros_like(token)
     first = info[0]
     transposed(slot, kt, (k0, k1))
     for frame in (0, 1):
@@ -226,13 +227,17 @@
             return ANY_SPEC
         block, whole = entry
         base = offset if whole else 0
+        if block == SLOT and whole:
+            return pl.BlockSpec((FT, HD), lambda h, s, info: (s, h + base))
         if block == SLOT:
-            return pl.BlockSpec((FT, HD), lambda h, s, info: (s, h + base))
+            return pl.BlockSpec((None, FT, HD), lambda h, s, info: (h, s, 0))
         return pl.BlockSpec((FT, HD), lambda h, s, info: (block, h + base))
 
     out_specs, shapes = [], []
     for rows, dtype, block in outs:
-        shapes.append(jax.ShapeDtypeStruct((rows, heads * HD), dtype))
+        by_head = block == SLOT
+        shape = (heads, rows, HD) if by_head else (rows, heads * HD)
+        shapes.append(jax.ShapeDtypeStruct(shape, dtype))
         if block is None:
             out_specs.append(pl.BlockSpec((rows, HD), lambda h, s, info: (0, h)))
         else:
@@ -258,74 +263,64 @@
     )(info, *arrays)
 
 
-def pick(flag, taken, kept, tokens=()):
-    flag = jnp.reshape(flag, (1,)).astype(jnp.int32)
-    rows, width = taken.shape
-    turns = 3
-    block = rows // turns
-
-    def kernel(flag, taken, kept, *refs):
-        out = refs[-1]
-
-        @pl.when(flag[0] == 1)
-        def _():
-            out[...] = taken[...]
-
-        @pl.when(flag[0] == 0)
-        def _():
-            out[...] = kept[...]
-
-    def spec(index):
-        return pl.BlockSpec((block, width), index)
-
+def move(plan, arrays, rows, flag=None, tokens=()):
+    width = arrays[0].shape[1]
+    n = len(arrays)
+    slots = len({target for _, _, _, target in plan})
+
+    def kernel(flag, *refs):
+        sources = refs[:n]
+        out, token, buf, sem = refs[n + len(tokens) :]
+        token[...] = jnp.zeros_like(token)
+
+        def each(act):
+            for when, source, row, target in plan:
+                slot = target // FT
+                copy = pltpu.make_async_copy(
+                    sources[source].at[pl.ds(row, FT)], buf.at[slot], sem.at[0, slot]
+                )
+                if when is None:
+                    act(copy)
+                else:
+                    pl.when(flag[0] == when)(lambda copy=copy: act(copy))
+
+        each(lambda copy: copy.start())
+        each(lambda copy: copy.wait())
+        outward = [
+            pltpu.make_async_copy(buf.at[slot], out.at[pl.ds(slot * FT, FT)], sem.at[1, slot])
+            for slot in range(slots)
+        ]
+        for copy in outward:
+            copy.start()
+        for copy in outward:
+            copy.wait()
+
+    flag = jnp.zeros((1,), jnp.int32) if flag is None else jnp.reshape(flag, (1,))
     return pl.pallas_call(
         kernel,
         grid_spec=pltpu.PrefetchScalarGridSpec(
             num_scalar_prefetch=1,
-            grid=(turns,),
-            in_specs=[
-                spec(lambda i, flag: (i * flag[0], 0)), spec(lambda i, flag: (i - i * flag[0], 0))
-            ] + [TOKEN_SPEC] * len(tokens),
-            out_specs=spec(lambda i, flag: (i, 0)),
+            grid=(1,),
+            in_specs=[ANY_SPEC] * n + [TOKEN_SPEC] * len(tokens),
+            out_specs=[ANY_SPEC, TOKEN_SPEC],
+            scratch_shapes=[
+                pltpu.VMEM((slots, FT, width), jnp.bfloat16), pltpu.SemaphoreType.DMA((2, slots))
+            ],
         ),
-        out_shape=jax.ShapeDtypeStruct((rows, width), taken.dtype),
+        out_shape=[jax.ShapeDtypeStruct((rows, width), jnp.bfloat16), TOKEN],
         compiler_params=PARAMS,
         cost_estimate=COST,
-    )(flag, taken, kept, *tokens)
-
-
-def last_frames(keys, values):
-    width = keys.shape[1]
-    turns = 4
-    block = 2 * FT // turns
-
-    def kernel(keys, values, out):
-        i = pl.program_id(0)
-
-        @pl.when(i < turns // 2)
-        def _():
-            out[...] = keys[...]
-
-        @pl.when(i >= turns // 2)
-        def _():
-            out[...] = values[...]
-
-    def spec(index):
-        return pl.BlockSpec((block, width), index)
-
-    half = turns // 2
-    return pl.pallas_call(
-        kernel,
-        grid=(turns,),
-        in_specs=[
-            spec(lambda i: (half + jnp.minimum(i, half - 1), 0)),
-            spec(lambda i: (jnp.maximum(i, half), 0)),
-        ],
-        out_specs=spec(lambda i: (i, 0)),
-        out_shape=jax.ShapeDtypeStruct((2 * FT, width), keys.dtype),
-        compiler_params=PARAMS,
-        cost_estimate=COST,
-    )(keys, values)
+    )(flag.astype(jnp.int32), *arrays, *tokens)
+
+
+def pick(flag, taken, kept, tokens=()):
+    plan = [(1, 0, 0, 0), (0, 1, 0, 0)]
+    return move(plan, [taken, kept], FT, flag, tokens)[0]
+
+
+def last_frames(keys, values, tokens=()):
+    plan = [(None, 0, FT, 0), (None, 1, FT, FT)]
+    return move(plan, [keys, values], 2 * FT, None, tokens)
 
 
 def sink_steps(size):
@@ -409,34 +404,43 @@
             [slot_all] + frames * 2, [(2 * FT, jnp.bfloat16, SLOT)] + sums, token=True,
         )
 
-    moved = lax.ppermute(value_states[:FT], axis, [(0, 1)])
-    held = pick(core, moved, key_states[:FT])
+    moved = lax.ppermute(value_states, axis, [(0, 1)])
+    held = pick(core, moved, key_states)
+    near_last, near_here = last_frames(near_k, near_v)
+    relay = lax.ppermute(near_last, axis, [(i, i + 1) for i in range(0, size, 2)])
+    own_last, _ = last_frames(key_states, value_states, [near_here])
+    far = lax.ppermute(own_last, axis, [(i, i + 2) for i in range(0, size - 2, 2)])
+
+    def near_stage(group, state):
+        return stage(
+            near_kernel, info, group, [query_states, near_k, near_k, near_v, near_v, *state],
+            [slot_all] + frames * 2 + [slot_part] * 3, sums, token=True,
+        )
+
     states = []
-    for step, pairs in enumerate(sink_steps(size)):
+    steps = sink_steps(size)
+    for step, pairs in enumerate(steps):
         moved = lax.ppermute(held, axis, pairs)
         tokens = []
         if step < len(groups):
             *state, token = local_stage(groups[step])
             states.append(state)
             tokens = [token]
+        if step == len(steps) - 2:
+            tokens.append(near_here)
+        if step == len(steps) - 1:
+            *sums_now, token = near_stage(groups[0], states[0])
+            states[0] = [states[0][0], *sums_now]
+            tokens.append(token)
         takes = jnp.zeros((), bool)
         for _, target in pairs:
             takes = takes | (me == target)
         held = pick(takes, moved, held, tokens)
     other = lax.ppermute(held, axis, [(i, i ^ 1) for i in range(size)])
 
-    own_last = last_frames(key_states, value_states)
-    far = lax.ppermute(own_last, axis, [(i, i + 2) for i in range(0, size - 2, 2)])
-    near_last = last_frames(near_k, near_v)
-    relay = lax.ppermute(near_last, axis, [(i, i + 1) for i in range(0, size, 2)])
-
-    for g, group in enumerate(groups):
-        m, acc, l = states[g]
-        acc, l = stage(
-            near_kernel, info, group, [query_states, near_k, near_k, near_v, near_v, m, acc, l],
-            [slot_all] + frames * 2 + [slot_part] * 3, sums,
-        )
-        states[g] = m, acc, l
+    for g, group in enumerate(groups[1:], 1):
+        *sums_now, _ = near_stage(group, states[g])
+        states[g] = [states[g][0], *sums_now]
     mine, theirs = [], []
     for g, group in enumerate(groups):
         outs = [(FT, jnp.bfloat16, 0)] * 2 if paired else [(2 * FT, jnp.bfloat16, None)]

time: 298 us -> 388 us (1.30)
  the two profiles are of different devices: /device:TPU:10 before, /device:TPU:2 now
where the time goes in v3:
time: 388 us; the launch traced here: 386 us
  Pallas kernels  327 us (84%)
  starting transfers between devices  41.8 us (11%)
  waiting for transfers between devices  10.8 us (3%)
  local copies, waits for them, and re-layouts  5.76 us (1%)
    pallas_call x6, Pallas kernels, stage(): pl.pallas_call(kernel, grid_spec=pltpu.PrefetchScalarGridSpec(num_scalar_...  299 us
    ppermute x1, starting transfers between devices, local(): lax.ppermute(near_last, axis, [(i, i + 1) for i in range(0, size, 2)])  21.3 us
    pallas_call x6, Pallas kernels, move(): pl.pallas_call(kernel, grid_spec=pltpu.PrefetchScalarGridSpec(num_scalar_...  19.7 us
    pallas_call x1, Pallas kernels, project(): pl.pallas_call(kernel, grid_spec=pltpu.PrefetchScalarGridSpec(num_scalar_...  8.01 us
  transfers between devices with their start and end apart: 11, of which 2 were waited for; matrix products, arithmetic and copies ran while one was open for 0% of the time, Pallas kernels for 48%

profile of v3, /device:TPU:2, one launch (start us, length us, event | category | flops | bytes accessed | tf_op | source)
XLA Modules:
  0.0 385.6 jit_solution(8302540699662758977)
XLA Ops:
  0.0 1.8 collective-permute-start
  1.8 1.9 collective-permute-start.4
  3.7 3.6 collective-permute-start.3
  7.3 2.7 shard_map.64
  10.0 1.6 collective-permute-start.1
  12.3 10.0 %shard_map.65 = (bf16[2,1536,128]{2,1,0:T(8,128)(2,1)}, f32[2,1536,128]{2,1,0:T(8,128)}, f32[2,1536,128]{2,1,0:T(8,128)}, f32[8,128]{1,0:T(8,128)}) custom-call(s32[7]{0:T(128)} %concatenate.3.info.refs_0_, bf16[1536,512]{1,0:T(8,128)(2,1)} %refs_1_.7, bf16[1536,512]{1,0:T(8,128)(2,1)} %refs_11_.3, bf16[1536,512]{1,0:T(8,128)(2,1)} %refs_11_.3, ...), custom_call_target="tpu_custom_call" | custom-call | flops 1000 | bytes 1000 | tf_op jit(solution)/shard_map/pallas_call | solution.py:245
  22.3 3.3 shard_map.66
  25.6 1.6 collective-permute-start.2
  27.2 10.1 %shard_map.67 = (bf16[2,1536,128]{2,1,0:T(8,128)(2,1)}, f32[2,1536,128]{2,1,0:T(8,128)}, f32[2,1536,128]{2,1,0:T(8,128)}, f32[8,128]{1,0:T(8,128)}) custom-call(s32[7]{0:T(128)} %concatenate.3.info.refs_0_, bf16[1536,512]{1,0:T(8,128)(2,1)} %refs_1_.7, bf16[1536,512]{1,0:T(8,128)(2,1)} %refs_11_.3, bf16[1536,512]{1,0:T(8,128)(2,1)} %refs_11_.3, ...), custom_call_target="tpu_custom_call" | custom-call | flops 1000 | bytes 1000 | tf_op jit(solution)/shard_map/pallas_call | solution.py:245
  37.3 3.3 collective-permute-done.3.refs_0_.k0.k1.refs_13_
  42.9 3.2 shard_map.68
  46.1 3.9 shard_map.72
  50.0 3.4 shard_map.69
  53.3 1.3 collective-permute-start.5
  54.6 6.4 %collective-permute-start.7 = (bf16[1536,512]{1,0:T(8,128)(2,1)}, bf16[1536,512]{1,0:T(8,128)(2,1)S(1)}, u32[]{:S(2)}, u32[]{:S(2)}) collective-permute-start(bf16[1536,512]{1,0:T(8,128)(2,1)} %get-tuple-element.40), channel_id=1, source_target_pairs={{0,4},{4,8},{8,12},{12,16},{16,20},{20,24},{24,28},{1,5},{5,9},{9,... | collective-permute-start | bytes 4718600 | tf_op jit(solution)/shard_map/ppermute | solution.py:412
  61.1 21.3 %collective-permute-start.8 = (bf16[1536,512]{1,0:T(8,128)(2,1)}, bf16[1536,512]{1,0:T(8,128)(2,1)S(1)}, u32[]{:S(2)}, u32[]{:S(2)}) collective-permute-start(bf16[1536,512]{1,0:T(8,128)(2,1)} %get-tuple-element.41), channel_id=1, source_target_pairs={{0,2},{4,6},{8,10},{12,14},{16,18},{20,22},{24,26},{28,30},{1,3},{... | collective-permute-start | bytes 4718600 | tf_op jit(solution)/shard_map/ppermute | solution.py:410
  82.5 10.0 %shard_map.70 = (f32[2,1536,128]{2,1,0:T(8,128)}, f32[2,1536,128]{2,1,0:T(8,128)}, f32[8,128]{1,0:T(8,128)}) custom-call(s32[7]{0:T(128)} %concatenate.3.info.refs_0_, bf16[1536,512]{1,0:T(8,128)(2,1)} %refs_1_.7, bf16[1536,512]{1,0:T(8,128)(2,1)} %copy-done.1, bf16[1536,512]{1,0:T(8,128)(2,1)} %copy-done.1, bf16[1536,512]{1,0:T(8,128)(2,1)} %copy-done, ...), custom_call_target="tpu_custom_call" | custom-call | flops 1000 | bytes 1000 | tf_op jit(solution)/shard_map/pallas_call | solution.py:245
  92.4 3.3 shard_map.71
  95.9 10.0 %shard_map.74 = (f32[2,1536,128]{2,1,0:T(8,128)}, f32[2,1536,128]{2,1,0:T(8,128)}, f32[8,128]{1,0:T(8,128)}) custom-call(s32[7]{0:T(128)} %concatenate.3.info.refs_0_, bf16[1536,512]{1,0:T(8,128)(2,1)} %refs_1_.7, bf16[1536,512]{1,0:T(8,128)(2,1)} %copy-done.1, bf16[1536,512]{1,0:T(8,128)(2,1)} %copy-done.1, bf16[1536,512]{1,0:T(8,128)(2,1)} %copy-done, ...), custom_call_target="tpu_custom_call" | custom-call | flops 1000 | bytes 1000 | tf_op jit(solution)/shard_map/pallas_call | solution.py:245
  107.8 129.6 %shard_map.75 = (bf16[768,256]{1,0:T(8,128)(2,1)}, bf16[768,256]{1,0:T(8,128)(2,1)}) custom-call(s32[7]{0:T(128)} %concatenate.3.info.refs_0_, bf16[1536,512]{1,0:T(8,128)(2,1)} %refs_1_.7, bf16[768,512]{1,0:T(8,128)(2,1)} %get-tuple-element.39.refs_2_.refs_15_, bf16[768,512]{1,0:T(8,128)(2,1)} %copy-done.4, bf16[1536,512]{1,0:T(8,128)(2,1)} %copy-done.2, ...), custom_call_target="tpu_custom_call" | custom-call | flops 1000 | bytes 1000 | tf_op jit(solution)/shard_map/pallas_call | solution.py:245
  237.4 1.6 collective-permute-start.10
  239.0 129.8 %shard_map.73 = (bf16[768,256]{1,0:T(8,128)(2,1)}, bf16[768,256]{1,0:T(8,128)(2,1)}) custom-call(s32[7]{0:T(128)} %concatenate.3.info.refs_0_, bf16[1536,512]{1,0:T(8,128)(2,1)} %refs_1_.7, bf16[768,512]{1,0:T(8,128)(2,1)} %get-tuple-element.39.refs_2_.refs_15_, bf16[768,512]{1,0:T(8,128)(2,1)} %copy-done.4, bf16[1536,512]{1,0:T(8,128)(2,1)} %copy-done.2, ...), custom_call_target="tpu_custom_call" | custom-call | flops 1000 | bytes 1000 | tf_op jit(solution)/shard_map/pallas_call | solution.py:245
  369.4 7.5 %collective-permute-done.9.refs_2_ = bf16[768,256]{1,0:T(8,128)(2,1)S(1)} collective-permute-done((bf16[768,256]{1,0:T(8,128)(2,1)}, bf16[768,256]{1,0:T(8,128)(2,1)S(1)}, u32[]{:S(2)}, u32[]{:S(2)}) %collective-permute-start.9) | collective-permute-done | bytes 393248 | tf_op jit(solution)/shard_map/ppermute | solution.py:456
  377.6 8.0 %shard_map.76 = bf16[768,1536]{1,0:T(8,128)(2,1)} custom-call(s32[7]{0:T(128)} %concatenate.3.info.refs_0_, bf16[768,256]{1,0:T(8,128)(2,1)} %get-tuple-element.44.refs_0_, bf16[768,256]{1,0:T(8,128)(2,1)} %get-tuple-element.50.refs_1_, bf16[768,256]{1,0:T(8,128)(2,1)} %copy-done.6, bf16[768,256]{1,0:T(8,128)(2,1)} %copy-done.5, bf16[1024,1536]{1,0:T(8,128)(2,1)} %refs_7_.1, ...), custom_call_target="tpu_custom_call" | custom-call | flops 1000 | bytes 1000 | tf_op jit(solution)/shard_map/pallas_call | solution.py:361
  (30 shorter events, 6.4 us)
Async XLA Ops:
  0.0 7.3 %collective-permute-start = (bf16[1536,512]{1,0:T(8,128)(2,1)}, bf16[1536,512]{1,0:T(8,128)(2,1)}, u32[]{:S(2)}, u32[]{:S(2)}) collective-permute-start(bf16[1536,512]{1,0:T(8,128)(2,1)} %refs_12_.3), channel_id=1, source_target_pairs={{0,2},{1,3}} | collective-permute-start | bytes 4718600 | tf_op jit(solution)/shard_map/ppermute | solution.py:407
  1.8 38.8 %collective-permute-start.4 = (bf16[1536,512]{1,0:T(8,128)(2,1)}, bf16[1536,512]{1,0:T(8,128)(2,1)S(1)}, u32[]{:S(2)}, u32[]{:S(2)}) collective-permute-start(bf16[1536,512]{1,0:T(8,128)(2,1)} %refs_12_.3), channel_id=1, source_target_pairs={{0,2},{2,4},{4,6},{6,8},{8,10},{10,12},{12,14},{14,16},{16,18},{18... | collective-permute-start | bytes 4718600 | tf_op jit(solution)/shard_map/ppermute | solution.py:398
  3.7 36.9 %collective-permute-start.3 = (bf16[1536,512]{1,0:T(8,128)(2,1)}, bf16[1536,512]{1,0:T(8,128)(2,1)S(1)}, u32[]{:S(2)}, u32[]{:S(2)}) collective-permute-start(bf16[1536,512]{1,0:T(8,128)(2,1)} %refs_11_.3), channel_id=1, source_target_pairs={{0,2},{2,4},{4,6},{6,8},{8,10},{10,12},{12,14},{14,16},{16,18},{18... | collective-permute-start | bytes 4718600 | tf_op jit(solution)/shard_map/ppermute | solution.py:397
  7.3 4.3 %copy-start.7 = (s32[2]{0:T(128)S(1)}, s32[2]{0:T(128)}, u32[]{:S(2)}) copy-start(s32[2]{0:T(128)} %param.9) | copy-start | bytes 28
  7.3 4.3 %copy-start.8 = (s32[2]{0:T(128)S(1)}, s32[2]{0:T(128)}, u32[]{:S(2)}) copy-start(s32[2]{0:T(128)} %param.10) | copy-start | bytes 28
  10.0 12.3 %collective-permute-start.1 = (bf16[768,512]{1,0:T(8,128)(2,1)}, bf16[768,512]{1,0:T(8,128)(2,1)}, u32[]{:S(2)}, u32[]{:S(2)}) collective-permute-start(bf16[768,512]{1,0:T(8,128)(2,1)} %get-tuple-element.29.refs_1_), channel_id=1, source_target_pairs={{0,16},{2,6},{1,17},{3,7}} | collective-permute-start | bytes 2359304 | tf_op jit(solution)/shard_map/ppermute | solution.py:423
  25.6 24.3 %collective-permute-start.2 = (bf16[768,512]{1,0:T(8,128)(2,1)}, bf16[768,512]{1,0:T(8,128)(2,1)}, u32[]{:S(2)}, u32[]{:S(2)}) collective-permute-start(bf16[768,512]{1,0:T(8,128)(2,1)} %get-tuple-element.31.refs_1_), channel_id=1, source_target_pairs={{0,8},{16,24},{2,18},{6,22},{1,9},{17,25},{3,19},{7,23}} | collective-permute-start | bytes 2359304 | tf_op jit(solution)/shard_map/ppermute | solution.py:423
  40.6 1.2 copy-start.1
  41.8 1.2 copy-start
  53.3 39.1 %collective-permute-start.5 = (bf16[768,512]{1,0:T(8,128)(2,1)}, bf16[768,512]{1,0:T(8,128)(2,1)}, u32[]{:S(2)}, u32[]{:S(2)}) collective-permute-start(bf16[768,512]{1,0:T(8,128)(2,1)} %get-tuple-element.34.refs_1_), channel_id=1, source_target_pairs={{0,4},{8,12},{16,20},{24,28},{2,10},{6,14},{18,26},{22,30},{1,5},{... | collective-permute-start | bytes 2359304 | tf_op jit(solution)/shard_map/ppermute | solution.py:423
  54.6 51.2 %collective-permute-start.7 = (bf16[1536,512]{1,0:T(8,128)(2,1)}, bf16[1536,512]{1,0:T(8,128)(2,1)S(1)}, u32[]{:S(2)}, u32[]{:S(2)}) collective-permute-start(bf16[1536,512]{1,0:T(8,128)(2,1)} %get-tuple-element.40), channel_id=1, source_target_pairs={{0,4},{4,8},{8,12},{12,16},{16,20},{20,24},{24,28},{1,5},{5,9},{9,... | collective-permute-start | bytes 4718600 | tf_op jit(solution)/shard_map/ppermute | solution.py:412
  61.1 44.7 %collective-permute-start.8 = (bf16[1536,512]{1,0:T(8,128)(2,1)}, bf16[1536,512]{1,0:T(8,128)(2,1)S(1)}, u32[]{:S(2)}, u32[]{:S(2)}) collective-permute-start(bf16[1536,512]{1,0:T(8,128)(2,1)} %get-tuple-element.41), channel_id=1, source_target_pairs={{0,2},{4,6},{8,10},{12,14},{16,18},{20,22},{24,26},{28,30},{1,3},{... | collective-permute-start | bytes 4718600 | tf_op jit(solution)/shard_map/ppermute | solution.py:410
  95.8 10.1 %collective-permute-start.6 = (bf16[768,512]{1,0:T(8,128)(2,1)}, bf16[768,512]{1,0:T(8,128)(2,1)S(1)}, u32[]{:S(2)}, u32[]{:S(2)}) collective-permute-start(bf16[768,512]{1,0:T(8,128)(2,1)} %get-tuple-element.39.refs_2_.refs_15_), channel_id=1, source_target_pairs={{0,2},{2,0},{4,6},{6,4},{8,10},{10,8},{12,14},{14,12},{16,18},{18,... | collective-permute-start | bytes 2359304 | tf_op jit(solution)/shard_map/ppermute | solution.py:439
  105.8 1.1 copy-start.2
  105.9 1.6 copy-start.3
  105.9 2.0 copy-start.4
  237.4 131.9 %collective-permute-start.10 = (bf16[768,256]{1,0:T(8,128)(2,1)}, bf16[768,256]{1,0:T(8,128)(2,1)S(1)}, u32[]{:S(2)}, u32[]{:S(2)}) collective-permute-start(bf16[768,256]{1,0:T(8,128)(2,1)} %get-tuple-element.52), channel_id=1, source_target_pairs={{0,1},{1,0},{2,3},{3,2},{4,5},{5,4},{6,7},{7,6},{8,9},{9,8},{10,11... | collective-permute-start | bytes 1179656 | tf_op jit(solution)/shard_map/ppermute | solution.py:456
  368.8 8.1 %collective-permute-start.9 = (bf16[768,256]{1,0:T(8,128)(2,1)}, bf16[768,256]{1,0:T(8,128)(2,1)S(1)}, u32[]{:S(2)}, u32[]{:S(2)}) collective-permute-start(bf16[768,256]{1,0:T(8,128)(2,1)} %get-tuple-element.51), channel_id=1, source_target_pairs={{0,1},{1,0},{2,3},{3,2},{4,5},{5,4},{6,7},{7,6},{8,9},{9,8},{10,11... | collective-permute-start | bytes 1179656 | tf_op jit(solution)/shard_map/ppermute | solution.py:456
  369.4 7.5 %copy-start.5 = (bf16[768,256]{1,0:T(8,128)(2,1)}, bf16[768,256]{1,0:T(8,128)(2,1)S(1)}, u32[]{:S(2)}) copy-start(bf16[768,256]{1,0:T(8,128)(2,1)S(1)} %collective-permute-done.10.refs_3_) | copy-start | bytes 1179652
  376.8 0.8 copy-start.6
